TPU v7x, 256 devices: a whole 4x4x8 slice. The times are simulated.
256 devices in a mesh: grp: 8 (over x_hi, y), dp: 32 (over x_lo, z, core).
Axes of the slice: x: 4 (x_hi: 2, x_lo: 2; x = x_hi * 2 + x_lo), y: 4, z: 8, core: 2. Of those that a mesh axis runs over, the one named last changes fastest.
Arguments:
- gradient_tiles: bfloat16 [8, 1536, 1536], P('grp', 'dp'), may hold values from -1.5 to 1.5
- qa_basis: bfloat16 [8, 2, 1536, 1536], P('grp', None, 'dp'), may hold values from -0.15625 to 0.15625
- qg_basis: bfloat16 [8, 2, 16, 1536, 1536], P('grp', None, None, None, 'dp'), may hold values from -0.15625 to 0.15625
- qa_values: bfloat16 [8, 2, 1536], P('grp'), may hold values from 0.29882812 to 3
- qg_values: bfloat16 [8, 2, 16, 1536], P('grp'), may hold values from 0.29882812 to 3
- layer_owner: int32 [2], replicated, may hold values from 0 to 7
- block_assign: int32 [2, 4], replicated, may hold values from 0 to 15
Outputs:
- preconditioned: bfloat16 [8, 1536, 1536], P('grp')
All inputs are finite; a program needn't handle non-finite values.
Results may differ from a plain program's by a relative error of at most 0.0065.
Values may be sent and summed in bfloat16 or wider, within the bound.
A program may use at most 128 MiB of HBM per device.

v0:
```python
import jax
import jax.numpy as jnp
from jax import lax
from jax.sharding import PartitionSpec as P

DAMPING = 0.1


def broadcast(value, axis, root):
    mine = lax.axis_index(axis) == root
    return lax.psum(jnp.where(mine, value, jnp.zeros_like(value)), axis)


def local(gradient_tiles, qa_basis, qg_basis, qa_values, qg_values, layer_owner, block_assign):
    layers = layer_owner.shape[0]
    blocks = block_assign.shape[1]
    width = gradient_tiles.shape[1]
    member = lax.axis_index("grp")
    mine_layer = member // blocks
    mine_slot = member % blocks
    own_start = lax.axis_index("dp") * width
    chosen = (
        jnp.zeros_like(qa_basis[0, 0]),
        jnp.zeros_like(qg_basis[0, 0]),
        jnp.zeros_like(qa_values[0, 0]),
        jnp.zeros_like(qg_values[0, 0]),
    )
    for layer_index in range(layers):
        arrived = (
            broadcast(qa_basis[0, layer_index], "grp", layer_owner[layer_index]),
            broadcast(qg_basis[0, layer_index], "grp", layer_owner[layer_index]),
            broadcast(qa_values[0, layer_index], "grp", layer_owner[layer_index]),
            broadcast(qg_values[0, layer_index], "grp", layer_owner[layer_index]),
        )
        picked = mine_layer == layer_index
        chosen = jax.tree.map(lambda fresh, older: jnp.where(picked, fresh, older), arrived, chosen)
    input_strip, output_strips, input_values, output_values = chosen
    block_index = block_assign[mine_layer, mine_slot]
    output_columns = output_strips[block_index]
    output_eigen = output_values[block_index]
    input_basis = lax.all_gather(input_strip, "dp", axis=0, tiled=True)
    rotated_in = jnp.dot(gradient_tiles[0], input_basis, preferred_element_type=jnp.float32).astype(
        jnp.bfloat16
    )
    basis_rows = output_columns
    eigen_coords = lax.dot_general(
        basis_rows,
        lax.all_gather(rotated_in, "dp", axis=0, tiled=True),
        (((0,), (0,)), ((), ())),
        preferred_element_type=jnp.float32,
    )
    own_eigen = lax.dynamic_slice_in_dim(output_eigen, own_start, width, 0).astype(jnp.float32)
    denominator = own_eigen[:, None] * input_values.astype(jnp.float32)[None, :] + DAMPING
    scaled = (eigen_coords / denominator).astype(jnp.bfloat16)
    back_in = lax.dot_general(
        scaled, input_basis, (((1,), (1,)), ((), ())), preferred_element_type=jnp.float32
    ).astype(jnp.bfloat16)
    basis_rows = output_columns
    result_rows = lax.psum_scatter(
        jnp.dot(basis_rows, back_in, preferred_element_type=jnp.float32),
        "dp",
        scatter_dimension=0,
        tiled=True,
    )
    finished = result_rows.astype(jnp.bfloat16)[None]
    return lax.all_gather(finished, "dp", axis=1, tiled=True)


def solution(mesh):
    in_specs = (
        P("grp", "dp", None),
        P("grp", None, "dp", None),
        P("grp", None, None, None, "dp"),
        P("grp", None, None),
        P("grp", None, None, None),
        P(),
        P(),
    )
    out_specs = P("grp", None, None)
    return jax.shard_map(local, mesh=mesh, in_specs=in_specs, out_specs=out_specs, check_vma=False)
```

profile of v0, /device:TPU:3, one launch (start us, length us, event | category | flops | bytes accessed | tf_op | source)
XLA Modules:
  0.0 593.3 jit_solution(13363898389552353480)
XLA Ops:
  6.5 1.3 fusion.15
  9.2 1.7 select_bitcast_fusion.2
  10.9 4.9 select_bitcast_fusion
  15.8 0.0 all-reduce.7.cloned.1.call-update
  15.8 0.0 all-gather.5.cloned.1.call-start
  15.9 131.2 %all-reduce.7.cloned.1.call-done = (bf16[48,1536]{1,0:T(8,128)(2,1)}, bf16[48,1536]{1,0:T(8,128)(2,1)}, bf16[16,1536,48]{1,2,0:T(8,128)(2,1)}, bf16[16,1536,48]{1,2,0:T(8,128)(2,1)}) async-done(((bf16[48,1536]{1,0:T(8,128)(2,1)}, bf16[48,1536]{1,0:T(8,128)(2,1)}, bf16[16,1536,48]{1,2,0:T(8,128)(2,1)}, bf16[16,1536,48]{1,2,0:T(8,128)(2,1)}), (bf16[48,1536]{1,0:T(8,128)(2,1)}, bf16[48,1536]{1,0:T(8,128)(2,1)}, ...) | async-done | bytes 5013520 | tf_op jit(solution)/shard_map/psum | solution.py:11
  147.1 1.6 select_select_fusion
  148.7 0.0 all-gather.5.cloned.1.call-update
  148.8 0.0 all-reduce.5.cloned.1.call-start
  148.8 0.6 fusion.6
  149.4 0.7 select_bitcast_fusion.4
  150.1 0.0 all-reduce.5.cloned.1.call-update
  150.1 0.0 copy-start.3
  150.1 0.0 all-gather.7.cloned.1.call-start
  150.2 65.6 %all-gather.5.cloned.1.call-done = bf16[1536,1536]{1,0:T(8,128)(2,1)} async-done(((bf16[48,1536]{1,0:T(8,128)(2,1)}), bf16[1536,1536]{1,0:T(8,128)(2,1)}) %all-gather.5.cloned.1.call-update) | async-done | bytes 4718608 | tf_op jit(solution)/shard_map/all_gather | solution.py:41
  215.8 3.9 fusion.1
  219.8 0.0 all-gather.7.cloned.1.call-update
  219.8 0.0 reduce-scatter.2.cloned.1.call-start
  219.9 0.7 dynamic_slice.10
  222.4 77.4 %all-reduce.5.cloned.1.call-done = (bf16[1536]{0:T(1024)(128)(2,1)}, bf16[1536]{0:T(1024)(128)(2,1)}, bf16[16,1536]{1,0:T(8,128)(2,1)}, bf16[16,1536]{1,0:T(8,128)(2,1)}) async-done(((bf16[1536]{0:T(1024)(128)(2,1)}, bf16[1536]{0:T(1024)(128)(2,1)}, bf16[16,1536]{1,0:T(8,128)(2,1)}, bf16[16,1536]{1,0:T(8,128)(2,1)}), (bf16[1536]{0:T(1024)(128)(2,1)}, bf16[1536]{0:T(1024)(128)(2,1)}, ...) | async-done | bytes 104464 | tf_op jit(solution)/shard_map/psum | solution.py:11
  299.8 0.8 fusion.10
  300.6 0.7 select_convert_fusion
  301.2 71.9 %all-gather.7.cloned.1.call-done = bf16[1536,1536]{1,0:T(8,128)(2,1)} async-done(((bf16[48,1536]{1,0:T(8,128)(2,1)}), bf16[1536,1536]{1,0:T(8,128)(2,1)}) %all-gather.7.cloned.1.call-update) | async-done | bytes 4718608 | tf_op jit(solution)/shard_map/all_gather | solution.py:48
  373.1 3.4 fusion
  376.5 8.9 %fusion.2 = f32[1536,1536]{1,0:T(8,128)} fusion(bf16[48,1536]{1,0:T(8,128)(2,1)S(1)} %fusion, bf16[1536,1536]{1,0:T(8,128)(2,1)} %all-gather.5.cloned.1.call-done, bf16[16,1536,48]{1,2,0:T(8,128)(2,1)} %get-tuple-element.13, s32[]{:T(128)S(6)} %select_n.170, bf16[16,1536,48]{1,2,0:T(8,128)(2,1)} %get-tuple-element.14, pred[]{:T(512)S(6)} %eq.10, pred[]{:T(512)S(6)} %eq.22), kind=kOutput, calls=%fused_computation.7 | convolution fusion | flops 453206016 | bytes 14598150 | tf_op jit(solution)/shard_map/dot_general | solution.py:60
  385.4 0.0 reduce-scatter.2.cloned.1.call-update
  385.4 0.0 all-gather.9.cloned.1.call-start
  385.5 126.5 %reduce-scatter.2.cloned.1.call-done = f32[48,1536]{1,0:T(8,128)} async-done(((f32[1536,1536]{1,0:T(8,128)}), f32[48,1536]{1,0:T(8,128)}) %reduce-scatter.2.cloned.1.call-update) | async-done | bytes 294928 | tf_op jit(solution)/shard_map/reduce_scatter | solution.py:59
  512.0 1.6 convert_element_type.35
  513.6 0.0 all-gather.9.cloned.1.call-update
  513.6 68.0 %all-gather.9.cloned.1.call-done = bf16[1536,1536]{1,0:T(8,128)(2,1)} async-done(((bf16[48,1536]{1,0:T(8,128)(2,1)}), bf16[1536,1536]{1,0:T(8,128)(2,1)}) %all-gather.9.cloned.1.call-update) | async-done | bytes 4718608 | tf_op jit(solution)/shard_map/all_gather | solution.py:66
  581.6 4.8 copy.17
  (8 shorter events, 0.0 us)
Async XLA Ops:
  6.5 209.3 %copy-start = (bf16[1,48,1536]{2,1,0:T(8,128)(2,1)S(1)}, bf16[1,48,1536]{2,1,0:T(8,128)(2,1)}, u32[]{:S(2)}) copy-start(bf16[1,48,1536]{2,1,0:T(8,128)(2,1)} %param.7) | copy-start | bytes 442372
  6.5 140.6 %all-reduce.7.cloned.1.call-start = ((), (), s32[]{:S(2)}) async-start(), calls=%async_computation.6 | async-start | bytes 10027008 | tf_op jit(solution)/shard_map/psum | solution.py:11
  15.8 133.0 %copy-start.2 = (bf16[1,2,1536]{2,1,0:T(2,128)(2,1)S(1)}, bf16[1,2,1536]{2,1,0:T(2,128)(2,1)}, u32[]{:S(2)}) copy-start(bf16[1,2,1536]{2,1,0:T(2,128)(2,1)} %param.10) | copy-start | bytes 18436
  15.8 133.6 %copy-start.1 = (bf16[1,2,16,1536]{3,2,1,0:T(8,128)(2,1)S(1)}, bf16[1,2,16,1536]{3,2,1,0:T(8,128)(2,1)}, u32[]{:S(2)}) copy-start(bf16[1,2,16,1536]{3,2,1,0:T(8,128)(2,1)} %param.11) | copy-start | bytes 294916
  15.8 200.0 %all-gather.5.cloned.1.call-start = ((), (), s32[]{:S(2)}) async-start(), calls=%async_computation.1 | async-start | bytes 4866048 | tf_op jit(solution)/shard_map/all_gather | solution.py:41
  148.8 151.0 %all-reduce.5.cloned.1.call-start = ((), (), s32[]{:S(2)}) async-start(), calls=%async_computation.5 | async-start | bytes 212992 | tf_op jit(solution)/shard_map/psum | solution.py:11
  150.1 69.7 %copy-start.3 = (s32[2,4]{1,0:T(2,128)S(1)}, s32[2,4]{1,0:T(2,128)}, u32[]{:S(2)}) copy-start(s32[2,4]{1,0:T(2,128)} %param.13) | copy-start | bytes 100
  150.1 223.0 %all-gather.7.cloned.1.call-start = ((), (), s32[]{:S(2)}) async-start(), calls=%async_computation.2 | async-start | bytes 4866048 | tf_op jit(solution)/shard_map/all_gather | solution.py:48
  219.8 292.2 %reduce-scatter.2.cloned.1.call-start = ((), (), s32[]{:S(2)}) async-start(), calls=%async_computation.3 | async-start | bytes 9732096 | tf_op jit(solution)/shard_map/reduce_scatter | solution.py:59
  385.4 196.2 %all-gather.9.cloned.1.call-start = ((), (), s32[]{:S(2)}) async-start(), calls=%async_computation.4 | async-start | bytes 4866048 | tf_op jit(solution)/shard_map/all_gather | solution.py:66
Sparse Core Ops, SparseCore 0:
  16.0 131.1 all-reduce.6
  149.1 66.6 all-gather.4
  219.0 80.7 all-reduce.4
  301.5 71.5 all-gather.6
  385.6 126.3 reduce-scatter.1
  513.8 67.8 all-gather.8
where the time goes:
time: 595 us; the launch traced here: 593 us
  waiting for transfers between devices  541 us (91%)
  between operations  16.8 us (3%)
  matrix products  16.2 us (3%)
  other arithmetic  12.6 us (2%)
  local copies, waits for them, and re-layouts  6.83 us (1%)
    psum x2, waiting for transfers between devices, broadcast(): return lax.psum(jnp.where(mine, value, jnp.zeros_like(value)), axis)  209 us
    reduce_scatter x1, waiting for transfers between devices, local(): lax.psum_scatter(jnp.dot(basis_rows, back_in, preferred_element_type=jnp....  126 us
    all_gather x1, waiting for transfers between devices, local(): lax.all_gather(rotated_in, 'dp', axis=0, tiled=True)  71.9 us
    all_gather x1, waiting for transfers between devices, local(): return lax.all_gather(finished, 'dp', axis=1, tiled=True)  68 us
    all_gather x1, waiting for transfers between devices, local(): input_basis = lax.all_gather(input_strip, 'dp', axis=0, tiled=True)  65.6 us
  transfers between devices with their start and end apart: 6, of which 6 were waited for; matrix products, arithmetic and copies ran while one was open for 1% of the time, Pallas kernels for 0%

commit v1 on v0

v1 whole, which is shorter than its diff:
```python
import functools

import jax
import jax.numpy as jnp
from jax import lax
from jax.experimental import pallas as pl
from jax.experimental.pallas import tpu as pltpu
from jax.sharding import PartitionSpec as P

MESH = pl.DeviceIdType.MESH
DAMPING = 0.1
NZ = 8
STRIP = 48
PIECE = 16
WIDTH = 1536
LANES = 128
N_DP = 32
HALF = WIDTH // 2
QUARTER = WIDTH // 4
TILE = 256
N_SEM = 256


def works(x, z):
    return (z + 2 * x) % 4 != 3


def rank(x, z):
    return x * 6 + z - (z + 2 * x) // 4


def kernel(
    owner_hbm, assign_hbm, g_hbm, a_hbm, q_hbm, lg_hbm, la_hbm, out_ref,
    owner_ref, assign_ref, lgv, lav, g, a, av, qv, qsel, qr_low, qr_high, qs, qt, qx, qc, ax, ay, vsel, vy, vx, vc, fg, fa, fq, p, lgc, sc, bp, bo, bi, bk, bc, bt,
    ssem, rsem, lsem, b_recv,
):
    member = lax.axis_index("grp")
    dp = lax.axis_index("dp")
    xh, y = member // 4, member % 4
    x, z, c = dp // 16, (dp // 2) % NZ, dp % 2

    load_g = [
        pltpu.make_async_copy(g_hbm.at[:, n * QUARTER:(n + 1) * QUARTER], g.at[n], lsem.at[7 + n]) for n in range(4)
    ]
    load_a = pltpu.make_async_copy(a_hbm, av, lsem.at[1])
    load_q = pltpu.make_async_copy(q_hbm, qv, lsem.at[2])
    loads = [
        pltpu.make_async_copy(src, dst, lsem.at[3 + n])
        for n, (src, dst) in enumerate(
            ((owner_hbm, owner_ref), (assign_hbm, assign_ref), (lg_hbm, lgv), (la_hbm, lav))
        )
    ]
    load_a.start()
    for load in load_g:
        load.start()
    for load in loads:
        load.start()
    load_q.start()
    core0 = c == 0

    def dev(gx, gy, dx, dz, dc):
        return (gx * 4 + gy, dx * 16 + dz * 2 + dc)

    sibling = dev(xh, y, x, z, 1 - c)
    across = dev(xh, y, 1 - x, z, c)
    up = dev(xh, y, x, (z + 1) % NZ, c)
    down = dev(xh, y, x, (z + NZ - 1) % NZ, c)
    across_other = dev(xh, y, 1 - x, z, 1 - c)
    up_other = dev(xh, y, x, (z + 1) % NZ, 1 - c)
    down_other = dev(xh, y, x, (z + NZ - 1) % NZ, 1 - c)
    partner = dev(1 - xh, y, x, z, c)

    barrier = pltpu.get_barrier_semaphore()

    near = [sibling, across, across_other, up, down, up_other, down_other, partner]
    near += [(xh * 4 + (y + k) % 4, dp) for k in range(1, 4)]
    for target in near:
        pl.semaphore_signal(barrier, inc=1, device_id=target, device_id_type=MESH)
    pl.semaphore_wait(barrier, len(near))

    count = [0]
    pending = []

    def number():
        count[0] += 1
        assert count[0] <= N_SEM
        return count[0] - 1

    def copy(m, src, dst, target):
        return pltpu.make_async_remote_copy(
            src_ref=src, dst_ref=dst, send_sem=ssem.at[m], recv_sem=rsem.at[m],
            device_id=target, device_id_type=MESH,
        )

    def send(m, src, dst, target, when=None):
        started = copy(m, src, dst, target)
        pending.append((started, when))
        if when is None:
            started.start()
        else:
            pl.when(when)(started.start)

    def drain(until=None):
        for started, when in pending[:until]:
            if when is None:
                started.wait_send()
            else:
                pl.when(when)(started.wait_send)
        del pending[:until]

    def arrive(m, dst, target, when=None):
        landed = copy(m, dst, dst, target)
        if when is None:
            landed.wait_recv()
        else:
            pl.when(when)(landed.wait_recv)

    class Gather:
        def __init__(self, ref, full, half=None, exists=None):
            self.ref, self.full, self.cut, self.mid = ref, full, full // 2, full // 4
            self.half = half or (lambda bx, bz, bc, to: ref(bx, bz, bc, 0, full))
            self.exists = exists or (lambda bx, bz: None)
            self.sib_waits = []
            self.m = {}

        def key(self, *name):
            if name not in self.m:
                self.m[name] = number()
            return self.m[name]

        def to_sibling(self, bx, bz):
            m = number()
            ref = self.half(bx, bz, c, 1 - c)
            send(m, ref, ref, sibling, self.exists(bx, bz))
            self.sib_waits.append((m, self.half(bx, bz, 1 - c, c), self.exists(bx, bz)))

        def move(self, name, target, bx, bz, first, last):
            ref = self.ref(bx, bz, c, first, last)
            send(self.key(*name), ref, ref, target, self.exists(bx, bz))

        def wait(self, name, bx, bz, first, last, bc=c):
            arrive(self.key(*name), self.ref(bx, bz, bc, first, last), sibling, self.exists(bx, bz))

        def low(self, name, target, bx, bz):
            self.move(name, target, bx, bz, 0, self.cut)

        def high(self, name, target, bx, bz):
            self.move(name, target, bx, bz, self.cut, self.full)

        def wait_low(self, name, bx, bz):
            self.wait(name, bx, bz, 0, self.cut)

        def wait_high(self, name, bx, bz):
            self.wait(name, bx, bz, self.cut, self.full)

        def begin_low(self):
            self.low(("x", 0), across, x, z)
            self.low(("ul", 1), up, x, z)
            self.low(("dl", 1), down, x, z)

        def begin_high(self):
            self.high(("uh", 1), up, x, z)
            self.high(("dh", 1), down, x, z)
            self.high(("xh", 0), across, x, z)
            self.to_sibling(x, z)

        def begin(self):
            self.low(("x", 0), across, x, z)
            self.high(("uh", 1), up, x, z)
            self.high(("dh", 1), down, x, z)
            self.low(("ul", 1), up, x, z)
            self.low(("dl", 1), down, x, z)
            self.high(("xh", 0), across, x, z)
            self.paired = self.whole(x)

        def whole(self, bx):
            m = number()
            ref = self.ref(bx, z, c, 0, self.full)
            send(m, ref, ref, sibling)
            return m, self.ref(bx, z, 1 - c, 0, self.full)

        def swap(self):
            self.wait_low(("x", 0), 1 - x, z)
            self.low(("uq", 1), up, 1 - x, z)
            self.low(("dq", 1), down, 1 - x, z)

        def from_x(self):
            self.wait_high(("xh", 0), 1 - x, z)
            if self is gq:
                self.crossing = self.whole(1 - x)
            else:
                self.to_sibling(1 - x, z)

        def step(self, s):
            lo, hi = (z + NZ - s) % NZ, (z + s) % NZ
            self.wait_high(("uh", s), x, lo)
            self.high(("uh", s + 1), up, x, lo)
            self.high(("xu", s), across, x, lo)
            self.wait_high(("dh", s), x, hi)
            if s < 3:
                self.high(("dh", s + 1), down, x, hi)
            self.high(("xd", s), across, x, hi)
            self.wait_low(("ul", s), x, lo)
            if s < 3:
                self.low(("ul", s + 1), up, x, lo)
            self.wait_low(("dl", s), x, hi)
            self.low(("dl", s + 1), down, x, hi)
            self.wait_low(("uq", s), 1 - x, lo)
            if s < 3:
                self.low(("uq", s + 1), up, 1 - x, lo)
            else:
                self.move(("uq", 4), up, 1 - x, lo, 0, self.mid)
                self.move(("uc", 4), up_other, 1 - x, lo, 0, self.mid)
            self.wait_low(("dq", s), 1 - x, hi)
            if s < 3:
                self.low(("dq", s + 1), down, 1 - x, hi)
            else:
                self.move(("dq", 4), down, 1 - x, hi, self.mid, self.cut)
                self.move(("dc", 4), down_other, 1 - x, hi, self.mid, self.cut)
            self.to_sibling(x, lo)
            self.to_sibling(x, hi)
            if s == 2 and self is not gq:
                self.from_x()
            if s > 1:
                self.crossed(s - 1)

        def crossed(self, s):
            lo, hi = (z + NZ - s) % NZ, (z + s) % NZ
            self.wait_high(("xu", s), 1 - x, lo)
            self.to_sibling(1 - x, lo)
            self.wait_high(("xd", s), 1 - x, hi)
            self.to_sibling(1 - x, hi)

        def last(self):
            far = (z + 4) % NZ
            self.wait_high(("uh", 4), x, far)
            self.high(("xu", 4), across, x, far)
            self.high(("xc", 4), across_other, x, far)
            self.wait_low(("dl", 4), x, far)
            self.to_sibling(x, far)
            self.crossed(3)
            self.wait(("uq", 4), 1 - x, far, 0, self.mid)
            self.wait(("dq", 4), 1 - x, far, self.mid, self.cut)
            self.wait_high(("xu", 4), 1 - x, far)

        def end(self):
            far = (z + 4) % NZ
            for m, ref, when in self.sib_waits:
                arrive(m, ref, sibling, when)
            self.wait(("uc", 4), 1 - x, far, 0, self.mid, 1 - c)
            self.wait(("dc", 4), 1 - x, far, self.mid, self.cut, 1 - c)
            self.wait(("xc", 4), 1 - x, far, self.cut, self.full, 1 - c)

    def strip_at(bz, bc):
        return pl.ds(pl.multiple_of((bz * 2 + bc) * STRIP, PIECE), STRIP)

    def strip_of(bz):
        return pl.ds(pl.multiple_of(bz * STRIP, PIECE), STRIP)

    def at_z(bz):
        return pl.ds(pl.multiple_of(bz * 2 * STRIP, PIECE), 2 * STRIP)

    def half_of(core):
        return pl.ds(pl.multiple_of(core * HALF, LANES), HALF)

    class Ring:
        def __init__(self, f):
            self.f = f
            self.m = {}
            self.m4 = [number() for _ in range(3)]

        def share(self, strip):
            self.f[x, strip_at(z, c), :] = strip[x * 2 + c]
            for n, (dx, dc) in enumerate(((1, 0), (1, 1), (0, 1))):
                bx, bc = (x + dx) % 2, (c + dc) % 2
                send(self.m4[n], strip.at[bx * 2 + bc], self.f.at[x, strip_at(z, c), :], dev(xh, y, bx, z, bc))

        def begin(self):
            for n, (dx, dc) in enumerate(((1, 0), (1, 1), (0, 1))):
                bx, bc = (x + dx) % 2, (c + dc) % 2
                arrive(self.m4[n], self.f.at[bx, strip_at(z, bc), :], sibling)
            for n in range(2):
                self.move("u", 1, n, up, z)
                self.move("d", 1, n, down, z)

        def move(self, way, s, n, target, bz):
            ref = self.f.at[n, at_z(bz), :]
            self.m[way, s, n] = number()
            send(self.m[way, s, n], ref, ref, target)

        def wait(self, way, s, n, bz):
            arrive(self.m[way, s, n], self.f.at[n, at_z(bz), :], sibling)

        def step(self, s):
            lo, hi = (z + NZ - s) % NZ, (z + s) % NZ
            for n in range(2):
                self.wait("u", s, n, lo)
                if s < 3 or n == 0:
                    self.move("u", s + 1, n, up, lo)
                self.wait("d", s, n, hi)
                if s < 3 or n == 1:
                    self.move("d", s + 1, n, down, hi)

        def last(self):
            far = (z + 4) % NZ
            self.wait("u", 4, 0, far)
            self.wait("d", 4, 1, far)

    def by_strips(bx, bz, bc, first, last):
        return fq.at[bc, bx, strip_of(bz), first:last]

    def by_columns(bx, bz, bc, first, last):
        cols = pl.ds(pl.multiple_of(rank(bx, bz) * LANES, LANES), LANES)
        return out_ref.at[pl.ds(pl.multiple_of(bc * HALF + first, PIECE), last - first), cols]

    gg = Ring(fg)
    ga = Ring(fa)
    gq = Gather(
        by_strips, WIDTH, half=lambda bx, bz, bc, to: fq.at[bc, bx, strip_of(bz), half_of(to)]
    )
    go = Gather(by_columns, HALF, exists=lambda bx, bz: works(bx, bz))

    own = pl.ds(pl.multiple_of(dp * STRIP, PIECE), STRIP)

    load_a.wait()
    m_ax = number()
    send(m_ax, av.at[1 - xh], ax.at[1], partner)
    for load in load_g:
        load.wait()
    gg.share(g)
    ax[0] = av[xh]

    for load in loads:
        load.wait()
    owner = owner_ref[xh]
    other = owner_ref[1 - xh]
    is_far = lax.bitwise_xor(lax.shift_right_logical(owner, 2), xh)
    owner_y = lax.bitwise_and(owner, 3)
    other_y = lax.bitwise_and(other, 3)
    load_q.wait()
    for layer in range(2):
        for slot in range(4):
            qsel[layer, slot] = qv[layer, assign_ref[layer, slot]]
    y_up, y_down = (xh * 4 + (y + 1) % 4, dp), (xh * 4 + (y + 3) % 4, dp)
    far, above, below = (y + 2) % 4, (y + 1) % 4, (y + 3) % 4
    m_q1, m_q2 = [number() for _ in range(2)], [number() for _ in range(2)]
    send(m_q1[0], qsel.at[:, far, :, :HALF], qr_low.at[:, 1], y_up)
    send(m_q1[1], qsel.at[:, far, :, HALF:], qr_high.at[:, 1], y_down)
    gg.begin()

    for layer in range(2):
        qr_low[layer, 0] = qsel[layer, above, :, :HALF]
        qr_high[layer, 0] = qsel[layer, below, :, HALF:]
        qt[layer, 0] = qsel[layer, y]
    owners_y = [lax.bitwise_and(owner_ref[layer], 3) for layer in range(2)]

    def one_if(condition):
        return jnp.where(condition, 1, 0)

    arrive(m_q1[0], qr_low.at[:, 1], y_down)
    for layer in range(2):
        qs[0, layer, :, :HALF] = qr_low[layer, one_if(owners_y[layer] == below)]
        qs[0, layer, :, HALF:] = qsel[layer, above, :, HALF:]
    send(m_q2[0], qs.at[0], qt.at[:, 1], y_up)
    arrive(m_q1[1], qr_high.at[:, 1], y_up)
    for layer in range(2):
        qs[1, layer, :, :HALF] = qsel[layer, below, :, :HALF]
        qs[1, layer, :, HALF:] = qr_high[layer, one_if(owners_y[layer] == above)]
    send(m_q2[1], qs.at[1], qt.at[:, 2], y_down)

    arrive(m_ax, ax.at[1], partner)
    ay[y] = ax[is_far]
    m_a1, m_a2 = [number() for _ in range(2)], [number() for _ in range(2)]
    send(m_a1[0], ay.at[y], ay.at[y], y_up)
    send(m_a1[1], ay.at[y], ay.at[y], y_down)

    m_vy = [number() for _ in range(3)]
    for layer in range(2):
        la_all = lav[...].astype(jnp.float32)[layer:layer + 1]
        lg_all = lgv[layer].astype(jnp.float32)
        at_row = lax.broadcasted_iota(jnp.int32, lg_all.shape, 0)
        for slot in range(4):
            lg = jnp.sum(jnp.where(at_row == assign_ref[layer, slot], lg_all, 0.0), axis=0, keepdims=True)
            for n in range(WIDTH // LANES):
                cols = slice(n * LANES, (n + 1) * LANES)
                vsel[slot, layer, 0, n:n + 1] = lg[:, cols]
                vsel[slot, layer, 1, n:n + 1] = la_all[:, cols]
    vy[y] = vsel[y]
    for k in range(1, 4):
        to = (y + k) % 4
        send(m_vy[k - 1], vsel.at[to], vy.at[y], (xh * 4 + to, dp))
    gg.step(1)
    arrive(m_a1[0], ay.at[below], y_down)
    send(m_a2[0], ay.at[below, :, :HALF], ay.at[below, :, :HALF], y_up)
    arrive(m_a1[1], ay.at[above], y_up)
    send(m_a2[1], ay.at[above, :, HALF:], ay.at[above, :, HALF:], y_down)
    gg.step(2)

    arrive(m_q2[0], qt.at[:, 1], y_down)
    arrive(m_q2[1], qt.at[:, 2], y_up)
    for k in range(1, 4):
        arrive(m_vy[k - 1], vy.at[(y + 4 - k) % 4], partner)

    def came(layer, column_half):
        away = lax.bitwise_and(lax.bitwise_and(owner_ref[layer], 3) + 4 - y, 3)
        by_below = (away >= 2) if column_half == 0 else (away == 3)
        return jnp.where(away == 0, 0, jnp.where(by_below, 1, 2))

    m_qx, m_vx = number(), number()
    for n in range(2):
        half = slice(n * HALF, (n + 1) * HALF)
        qc[:, half] = qt[1 - xh, came(1 - xh, n), :, half]
    send(m_qx, qc, qx.at[1], partner)
    vc[...] = vy[other_y, 1 - xh]
    send(m_vx, vc, vx.at[1], partner)
    for n in range(2):
        half = slice(n * HALF, (n + 1) * HALF)
        qx[0, :, half] = qt[xh, came(xh, n), :, half]
    vx[0] = vy[owner_y, xh]

    arrive(m_a2[0], ay.at[far, :, :HALF], y_down)
    arrive(m_a2[1], ay.at[far, :, HALF:], y_up)
    strip_a = ay[owner_y]
    for n in range(4):
        a[n] = strip_a[:, n * QUARTER:(n + 1) * QUARTER]
    ga.share(a)
    gg.step(3)
    arrive(m_qx, qx.at[1], partner)
    fq[c, x, strip_of(z), :] = qx[is_far]
    gq.begin()
    ga.begin()
    gg.last()
    gq.swap()
    arrive(m_vx, vx.at[1], partner)
    for n in range(WIDTH // LANES):
        lg_row = vx[is_far, 0, n:n + 1, :]
        lgc[n * LANES:(n + 1) * LANES, :] = jnp.transpose(jnp.broadcast_to(lg_row, (LANES, LANES)))
    ga.step(1)
    gq.from_x()
    gq.step(1)
    ga.step(2)

    arrive(*gq.paired, sibling)
    arrive(*gq.crossing, sibling)

    def flat(value):
        return value.reshape((-1, value.shape[-1]))

    p[x * 2 + c] = jnp.dot(
        flat(fq[:, :, strip_of(z), :]), flat(fg[...]), preferred_element_type=jnp.float32
    ).astype(jnp.bfloat16)
    m_p = [number() for _ in range(3)]
    p_own, p_far = p.at[x * 2 + c], p.at[(1 - x) * 2 + c]
    send(m_p[0], p_own, p_own, across)
    send(m_p[1], p_own, p_own, sibling)
    ga.step(3)
    arrive(m_p[0], p_far, across)
    send(m_p[2], p_far, p_far, sibling)
    gq.step(2)
    ga.last()

    arrive(m_p[1], p.at[x * 2 + 1 - c], sibling)
    arrive(m_p[2], p.at[(1 - x) * 2 + 1 - c], sibling)
    eigen = sum(
        jnp.dot(p[n], fa[n // 2, n % 2 * QUARTER:(n % 2 + 1) * QUARTER, :], preferred_element_type=jnp.float32)
        for n in range(4)
    )
    lg_col = jnp.concatenate([lgc[pl.ds(pl.multiple_of(bx * HALF + (z * 2 + bc) * STRIP, PIECE), STRIP), :]
                              for bc in range(2) for bx in range(2)])
    for n in range(QUARTER // LANES):
        la_row = vx[is_far, 1, pl.ds((x * 2 + c) * (QUARTER // LANES) + n, 1), :]
        cols = slice(n * LANES, (n + 1) * LANES)
        sc[:, cols] = (eigen[:, cols] / (lg_col * la_row + DAMPING)).astype(jnp.bfloat16)

    for bx in range(2):
        for n in range(2):
            rows = slice(n * QUARTER, (n + 1) * QUARTER)
            part = lax.dot_general(
                sc[...], fa[bx, rows, :], (((1,), (1,)), ((), ())), preferred_element_type=jnp.float32
            ).reshape((2, 2, STRIP, QUARTER))
            cols = slice(bx * HALF + n * QUARTER, bx * HALF + (n + 1) * QUARTER)
            bp[:, :, :, cols] = part
            bo[:, :, :, cols] = part.astype(jnp.bfloat16)
    m_b = number()
    send(m_b, bo.at[1 - c], bi, sibling)
    gq.step(3)
    arrive(m_b, bi, sibling)
    done = (bp[c] + bi[...].astype(jnp.float32)).astype(jnp.bfloat16)
    for j in range(WIDTH // LANES):
        bk[j] = done[:, :, j * LANES:(j + 1) * LANES]

    for wx in range(2):
        for wz in range(NZ):
            if (wz + 2 * wx) % 4 == 3:
                continue
            part = bk.at[wx * 6 + wz - (wz + 2 * wx) // 4]
            to_self = jnp.logical_and(x == wx, z == wz)
            others = jnp.logical_not(to_self)
            started = pltpu.make_async_remote_copy(
                src_ref=part, dst_ref=bc.at[x, :, strip_of(z), :], send_sem=ssem.at[number()],
                recv_sem=b_recv.at[x * NZ + z], device_id=dev(xh, y, wx, wz, c), device_id_type=MESH,
            )
            pl.when(others)(started.start)
            pending.append((started, others))

            @pl.when(to_self)
            def _():
                bc[x, :, strip_of(z), :] = part[...]

    gq.last()
    is_worker = works(x, z)
    m_bt = number()

    @pl.when(is_worker)
    def _():
        def take(k, carry):
            n = (x * NZ + z + k) % 16
            block = bc.at[n // NZ, :, strip_of(n % NZ), :]
            pltpu.make_async_remote_copy(
                src_ref=block, dst_ref=block, send_sem=ssem.at[m_bt], recv_sem=b_recv.at[n],
                device_id=sibling, device_id_type=MESH,
            ).wait_recv()
            return carry

        lax.fori_loop(1, 16, take, 0)
        total = flat(bc[0].astype(jnp.float32) + bc[1].astype(jnp.float32))
        for n in range(HALF // LANES):
            cols = slice(n * LANES, (n + 1) * LANES)
            bt[c, :, cols] = jnp.transpose(total[cols, :]).astype(jnp.bfloat16)

    send(m_bt, bt.at[c], bt.at[c], sibling, is_worker)
    gq.end()
    arrive(m_bt, bt.at[1 - c], sibling, is_worker)

    mine = pl.ds(pl.multiple_of(rank(x, z) * LANES, LANES), LANES)

    def finish(n):
        @pl.when(is_worker)
        def _():
            rows = pl.ds(pl.multiple_of(c * HALF + n * QUARTER, LANES), QUARTER)
            part = sum(
                jnp.dot(bt[k], flat(fq[k, :, :, rows]), preferred_element_type=jnp.float32) for k in range(2)
            )
            out_ref[rows, mine] = jnp.transpose(part).astype(jnp.bfloat16)

    finish(0)
    go.begin_low()
    finish(1)
    go.begin_high()
    drain()
    go.swap()
    go.step(1)
    early = len(pending)
    go.step(2)
    go.step(3)
    drain(early)
    go.last()
    go.end()
    drain()


def local(gradient_tiles, qa_basis, qg_basis, qa_values, qg_values, layer_owner, block_assign):
    strip = (STRIP, WIDTH)
    bf = jnp.bfloat16
    f32 = jnp.float32
    out = pl.pallas_call(
        kernel,
        out_shape=jax.ShapeDtypeStruct((WIDTH, WIDTH), bf),
        in_specs=[pl.BlockSpec(memory_space=pltpu.HBM)] * 7,
        out_specs=pl.BlockSpec(memory_space=pltpu.VMEM),
        scratch_shapes=[
            pltpu.SMEM((2,), jnp.int32),
            pltpu.SMEM((2, 4), jnp.int32),
            pltpu.VMEM((2, 16, WIDTH), bf),
            pltpu.VMEM((2, WIDTH), bf),
            pltpu.VMEM((4, STRIP, QUARTER), bf),
            pltpu.VMEM((4, STRIP, QUARTER), bf),
            pltpu.VMEM((2,) + strip, bf),
            pltpu.VMEM((2, 16) + strip, bf),
            pltpu.VMEM((2, 4) + strip, bf),
            pltpu.VMEM((2, 2, STRIP, HALF), bf),
            pltpu.VMEM((2, 2, STRIP, HALF), bf),
            pltpu.VMEM((2, 2) + strip, bf),
            pltpu.VMEM((2, 3) + strip, bf),
            pltpu.VMEM((2,) + strip, bf),
            pltpu.VMEM(strip, bf),
            pltpu.VMEM((2,) + strip, bf),
            pltpu.VMEM((4,) + strip, bf),
            pltpu.VMEM((4, 2, 2, 16, LANES), f32),
            pltpu.VMEM((4, 2, 2, 16, LANES), f32),
            pltpu.VMEM((2, 2, 16, LANES), f32),
            pltpu.VMEM((2, 16, LANES), f32),
            pltpu.VMEM((2, HALF, QUARTER), bf),
            pltpu.VMEM((2, HALF, QUARTER), bf),
            pltpu.VMEM((2, 2, HALF // 2, WIDTH), bf),
            pltpu.VMEM((4, 4 * STRIP, QUARTER), bf),
            pltpu.VMEM((WIDTH, LANES), f32),
            pltpu.VMEM((4 * STRIP, QUARTER), bf),
            pltpu.VMEM((2, 2) + strip, f32),
            pltpu.VMEM((2, 2) + strip, bf),
            pltpu.VMEM((2,) + strip, bf),
            pltpu.VMEM((12, 2, STRIP, LANES), bf),
            pltpu.VMEM((2, 2, HALF // 2, LANES), bf),
            pltpu.VMEM((2, LANES, HALF), bf),
            pltpu.SemaphoreType.DMA((N_SEM,)),
            pltpu.SemaphoreType.DMA((N_SEM,)),
            pltpu.SemaphoreType.DMA((11,)),
            pltpu.SemaphoreType.DMA((16,)),
        ],
        compiler_params=pltpu.CompilerParams(
            collective_id=0, has_side_effects=True, vmem_limit_bytes=48 * 1024 * 1024
        ),
        cost_estimate=pl.CostEstimate(flops=4 * 2 * 48 * 1536 * 1536, bytes_accessed=10_000_000, transcendentals=0),
    )(
        *(
            pltpu.with_memory_space_constraint(operand, pltpu.HBM)
            for operand in (
                layer_owner, block_assign, gradient_tiles[0], qa_basis[0], jnp.swapaxes(qg_basis[0], -1, -2),
                qg_values[0], qa_values[0],
            )
        )
    )
    return out[None]


def solution(mesh):
    in_specs = (
        P("grp", "dp", None),
        P("grp", None, "dp", None),
        P("grp", None, None, None, "dp"),
        P("grp", None, None),
        P("grp", None, None, None),
        P(),
        P(),
    )
    out_specs = P("grp", None, None)
    return jax.shard_map(local, mesh=mesh, in_specs=in_specs, out_specs=out_specs, check_vma=False)
```

time: 595 us -> 110 us (0.18)
  waiting for transfers between devices: 541 us -> 0 us
  Pallas kernels: 0 us -> 107 us
  between operations: 16.8 us -> 0.01 us
  matrix products: 16.2 us -> 0 us
  other arithmetic: 12.6 us -> 0 us
    psum x2 -> x0, waiting for transfers between devices: 209 us -> none  [broadcast(): return lax.psum(jnp.where(mine, value, jnp.zeros_like(value)), axis)]
    all_gather x3 -> x0, waiting for transfers between devices: 206 us -> none  [the longest x1 71.9 us: local(): lax.all_gather(rotated_in, 'dp', axis=0, tiled=True)]
    reduce_scatter x1 -> x0, waiting for transfers between devices: 126 us -> none  [local(): lax.psum_scatter(jnp.dot(basis_rows, back_in, preferred_element_type=jnp....]
    pallas_call x0 -> x1, Pallas kernels: none -> 107 us  [local(): pl.pallas_call(kernel, out_shape=jax.ShapeDtypeStruct((WIDTH, WIDTH), bf)...]
    dot_general x3 -> x0, matrix products: 16.2 us -> none  [the longest x1 8.89 us: local(): jnp.dot(basis_rows, back_in, preferred_element_type=jnp.float32)]
    select_n x5 -> x0, other arithmetic: 9.52 us -> none  [the longest x4 7.93 us: broadcast(): return lax.psum(jnp.where(mine, value, jnp.zeros_like(value)), axis)]
  transfers between devices with their start and end apart: 6 -> 0, of which waited for: 6 -> 0; matrix products, arithmetic and copies ran while one was open for 1% -> 0% of each run, Pallas kernels for 0% -> 0%
where the time goes in v1:
time: 110 us
  Pallas kernels  107 us (97%)
  local copies, waits for them, and re-layouts  2.19 us (2%)
    pallas_call x1, Pallas kernels, local(): pl.pallas_call(kernel, out_shape=jax.ShapeDtypeStruct((WIDTH, WIDTH), bf)...  107 us

profile of v1, /device:TPU:3, one launch (start us, length us, event | category | flops | bytes accessed | tf_op | source)
XLA Modules:
  0.0 109.5 jit_solution(6952191985907257166)
XLA Ops:
  0.0 107.3 %shard_map.73 = bf16[1536,1536]{1,0:T(8,128)(2,1)S(1)} custom-call(s32[2]{0:T(128)} %owner_hbm.1, s32[2,4]{1,0:T(2,128)} %assign_hbm.1, bf16[48,1536]{1,0:T(8,128)(2,1)} %bitcast.11, bf16[2,48,1536]{2,1,0:T(8,128)(2,1)} %bitcast.10, bf16[2,16,48,1536]{3,2,1,0:T(8,128)(2,1)} %bitcast.9, bf16[2,16,1536]{2,1,0:T(8,128)(2,1)} %bitcast.12, bf16[2,1536]{1,0:T(2,128)(2,1)} %bitcast.13), custom_call_target="tpu_custom_call" | custom-call | flops 905969664 | bytes 10000000 | tf_op jit(solution)/shard_map/pallas_call | solution.py:566
  107.3 2.2 %copy.9 = bf16[1,1536,1536]{2,1,0:T(8,128)(2,1)} copy(bf16[1,1536,1536]{2,1,0:T(8,128)(2,1)S(1)} %bitcast.8) | data formatting | bytes 9437184

commit v2 on v1

--- a/solution.py
+++ b/solution.py
@@ -31,8 +31,8 @@
 
 def kernel(
     owner_hbm, assign_hbm, g_hbm, a_hbm, q_hbm, lg_hbm, la_hbm, out_ref,
-    owner_ref, assign_ref, lgv, lav, g, a, av, qv, qsel, qr_low, qr_high, qs, qt, qx, qc, ax, ay, vsel, vy, vx, vc, fg, fa, fq, p, lgc, sc, bp, bo, bi, bk, bc, bt,
-    ssem, rsem, lsem, b_recv,
+    owner_ref, assign_ref, lgv, lav, g, av, qv, qsel, qr_low, qr_high, qs, qt, qx, qc, aq, ac, ax, vsel, vy, vx, vc, fg, fa, fq, p, lgc, sc, bp, bo, bi, bk, bc, bt,
+    ssem, rsem, lsem, a_recv, b_recv,
 ):
     member = lax.axis_index("grp")
     dp = lax.axis_index("dp")
@@ -42,7 +42,10 @@
     load_g = [
         pltpu.make_async_copy(g_hbm.at[:, n * QUARTER:(n + 1) * QUARTER], g.at[n], lsem.at[7 + n]) for n in range(4)
     ]
-    load_a = pltpu.make_async_copy(a_hbm, av, lsem.at[1])
+    load_a = [
+        pltpu.make_async_copy(a_hbm.at[:, :, n * QUARTER:(n + 1) * QUARTER], av.at[n], lsem.at[11 + n])
+        for n in range(4)
+    ]
     load_q = pltpu.make_async_copy(q_hbm, qv, lsem.at[2])
     loads = [
         pltpu.make_async_copy(src, dst, lsem.at[3 + n])
@@ -50,7 +53,8 @@
             ((owner_hbm, owner_ref), (assign_hbm, assign_ref), (lg_hbm, lgv), (la_hbm, lav))
         )
     ]
-    load_a.start()
+    for load in load_a:
+        load.start()
     for load in load_g:
         load.start()
     for load in loads:
@@ -58,8 +62,11 @@
     load_q.start()
     core0 = c == 0
 
+    def dp_of(dx, dz, dc):
+        return dx * 16 + dz * 2 + dc
+
     def dev(gx, gy, dx, dz, dc):
-        return (gx * 4 + gy, dx * 16 + dz * 2 + dc)
+        return (gx * 4 + gy, dp_of(dx, dz, dc))
 
     sibling = dev(xh, y, x, z, 1 - c)
     across = dev(xh, y, 1 - x, z, c)
@@ -72,8 +79,10 @@
 
     barrier = pltpu.get_barrier_semaphore()
 
-    near = [sibling, across, across_other, up, down, up_other, down_other, partner]
-    near += [(xh * 4 + (y + k) % 4, dp) for k in range(1, 4)]
+    near = [up, down, up_other, down_other, partner]
+    near += [
+        dev(xh, (y + k // 4) % 4, (x + k // 2) % 2, z, (c + k) % 2) for k in range(1, 16)
+    ]
     for target in near:
         pl.semaphore_signal(barrier, inc=1, device_id=target, device_id_type=MESH)
     pl.semaphore_wait(barrier, len(near))
@@ -314,7 +323,6 @@
         return out_ref.at[pl.ds(pl.multiple_of(bc * HALF + first, PIECE), last - first), cols]
 
     gg = Ring(fg)
-    ga = Ring(fa)
     gq = Gather(
         by_strips, WIDTH, half=lambda bx, bz, bc, to: fq.at[bc, bx, strip_of(bz), half_of(to)]
     )
@@ -322,13 +330,26 @@
 
     own = pl.ds(pl.multiple_of(dp * STRIP, PIECE), STRIP)
 
-    load_a.wait()
-    m_ax = number()
-    send(m_ax, av.at[1 - xh], ax.at[1], partner)
+    for load in load_a:
+        load.wait()
+    mine_a = x * 2 + c
+    in_place = mine_a == y
+    for n in range(4):
+        started = pltpu.make_async_remote_copy(
+            src_ref=av.at[n], dst_ref=aq.at[y], send_sem=ssem.at[number()], recv_sem=a_recv.at[y],
+            device_id=(xh * 4 + mine_a, dp_of(n // 2, z, n % 2)), device_id_type=MESH,
+        )
+        there = jnp.logical_not(jnp.logical_and(in_place, y == n))
+        pl.when(there)(started.start)
+        pending.append((started, there))
+
+    @pl.when(in_place)
+    def _():
+        aq[y] = av[y]
+
     for load in load_g:
         load.wait()
     gg.share(g)
-    ax[0] = av[xh]
 
     for load in loads:
         load.wait()
@@ -368,11 +389,24 @@
         qs[1, layer, :, HALF:] = qr_high[layer, one_if(owners_y[layer] == above)]
     send(m_q2[1], qs.at[1], qt.at[:, 2], y_down)
 
-    arrive(m_ax, ax.at[1], partner)
-    ay[y] = ax[is_far]
-    m_a1, m_a2 = [number() for _ in range(2)], [number() for _ in range(2)]
-    send(m_a1[0], ay.at[y], ay.at[y], y_up)
-    send(m_a1[1], ay.at[y], ay.at[y], y_down)
+    for k in range(1, 4):
+        m_a = (y + k) % 4
+        pltpu.make_async_remote_copy(
+            src_ref=aq.at[m_a], dst_ref=aq.at[m_a], send_sem=ssem.at[0], recv_sem=a_recv.at[m_a],
+            device_id=sibling, device_id_type=MESH,
+        ).wait_recv()
+
+    @pl.when(jnp.logical_not(in_place))
+    def _():
+        pltpu.make_async_remote_copy(
+            src_ref=aq.at[y], dst_ref=aq.at[y], send_sem=ssem.at[0], recv_sem=a_recv.at[y],
+            device_id=sibling, device_id_type=MESH,
+        ).wait_recv()
+
+    m_ax = number()
+    ac[...] = aq[other_y, 1 - xh]
+    send(m_ax, ac, ax.at[1], partner)
+    ax[0] = aq[owner_y, xh]
 
     m_vy = [number() for _ in range(3)]
     for layer in range(2):
@@ -390,10 +424,26 @@
         to = (y + k) % 4
         send(m_vy[k - 1], vsel.at[to], vy.at[y], (xh * 4 + to, dp))
     gg.step(1)
-    arrive(m_a1[0], ay.at[below], y_down)
-    send(m_a2[0], ay.at[below, :, :HALF], ay.at[below, :, :HALF], y_up)
-    arrive(m_a1[1], ay.at[above], y_up)
-    send(m_a2[1], ay.at[above, :, HALF:], ay.at[above, :, HALF:], y_down)
+    arrive(m_ax, ax.at[1], partner)
+    fa[y // 2, z, y % 2] = ax[is_far]
+    m_a = {}
+
+    def ring_a(way, s, bz):
+        ref = fa.at[y // 2, bz, y % 2]
+        m_a[way, s] = number()
+        send(m_a[way, s], ref, ref, up if way == "u" else down)
+
+    def step_a(s):
+        lo, hi = (z + NZ - s) % NZ, (z + s) % NZ
+        arrive(m_a["u", s], fa.at[y // 2, lo, y % 2], sibling)
+        if s < 4:
+            ring_a("u", s + 1, lo)
+            arrive(m_a["d", s], fa.at[y // 2, hi, y % 2], sibling)
+        if s < 3:
+            ring_a("d", s + 1, hi)
+
+    ring_a("u", 1, z)
+    ring_a("d", 1, z)
     gg.step(2)
 
     arrive(m_q2[0], qt.at[:, 1], y_down)
@@ -418,27 +468,32 @@
         qx[0, :, half] = qt[xh, came(xh, n), :, half]
     vx[0] = vy[owner_y, xh]
 
-    arrive(m_a2[0], ay.at[far, :, :HALF], y_down)
-    arrive(m_a2[1], ay.at[far, :, HALF:], y_up)
-    strip_a = ay[owner_y]
-    for n in range(4):
-        a[n] = strip_a[:, n * QUARTER:(n + 1) * QUARTER]
-    ga.share(a)
+    step_a(1)
     gg.step(3)
+    step_a(2)
     arrive(m_qx, qx.at[1], partner)
     fq[c, x, strip_of(z), :] = qx[is_far]
     gq.begin()
-    ga.begin()
+    step_a(3)
     gg.last()
+    step_a(4)
+    m_y1, m_y2 = [number() for _ in range(2)], [number() for _ in range(2)]
+    plane = fa.at[y // 2, :, y % 2]
+    send(m_y1[0], plane, plane, y_up)
+    send(m_y1[1], plane, plane, y_down)
     gq.swap()
     arrive(m_vx, vx.at[1], partner)
     for n in range(WIDTH // LANES):
         lg_row = vx[is_far, 0, n:n + 1, :]
         lgc[n * LANES:(n + 1) * LANES, :] = jnp.transpose(jnp.broadcast_to(lg_row, (LANES, LANES)))
-    ga.step(1)
     gq.from_x()
     gq.step(1)
-    ga.step(2)
+    arrive(m_y1[0], fa.at[below // 2, :, below % 2], sibling)
+    lower = fa.at[below // 2, 0:4, below % 2]
+    send(m_y2[0], lower, lower, y_up)
+    arrive(m_y1[1], fa.at[above // 2, :, above % 2], sibling)
+    upper = fa.at[above // 2, 4:8, above % 2]
+    send(m_y2[1], upper, upper, y_down)
 
     arrive(*gq.paired, sibling)
     arrive(*gq.crossing, sibling)
@@ -453,16 +508,16 @@
     p_own, p_far = p.at[x * 2 + c], p.at[(1 - x) * 2 + c]
     send(m_p[0], p_own, p_own, across)
     send(m_p[1], p_own, p_own, sibling)
-    ga.step(3)
     arrive(m_p[0], p_far, across)
     send(m_p[2], p_far, p_far, sibling)
     gq.step(2)
-    ga.last()
+    arrive(m_y2[0], fa.at[far // 2, 0:4, far % 2], sibling)
+    arrive(m_y2[1], fa.at[far // 2, 4:8, far % 2], sibling)
 
     arrive(m_p[1], p.at[x * 2 + 1 - c], sibling)
     arrive(m_p[2], p.at[(1 - x) * 2 + 1 - c], sibling)
     eigen = sum(
-        jnp.dot(p[n], fa[n // 2, n % 2 * QUARTER:(n % 2 + 1) * QUARTER, :], preferred_element_type=jnp.float32)
+        jnp.dot(p[n], flat(fa[n // 2, n % 2 * 4:n % 2 * 4 + 4]), preferred_element_type=jnp.float32)
         for n in range(4)
     )
     lg_col = jnp.concatenate([lgc[pl.ds(pl.multiple_of(bx * HALF + (z * 2 + bc) * STRIP, PIECE), STRIP), :]
@@ -474,9 +529,8 @@
 
     for bx in range(2):
         for n in range(2):
-            rows = slice(n * QUARTER, (n + 1) * QUARTER)
             part = lax.dot_general(
-                sc[...], fa[bx, rows, :], (((1,), (1,)), ((), ())), preferred_element_type=jnp.float32
+                sc[...], flat(fa[bx, n * 4:n * 4 + 4]), (((1,), (1,)), ((), ())), preferred_element_type=jnp.float32
             ).reshape((2, 2, STRIP, QUARTER))
             cols = slice(bx * HALF + n * QUARTER, bx * HALF + (n + 1) * QUARTER)
             bp[:, :, :, cols] = part
@@ -574,8 +628,7 @@
             pltpu.VMEM((2, 16, WIDTH), bf),
             pltpu.VMEM((2, WIDTH), bf),
             pltpu.VMEM((4, STRIP, QUARTER), bf),
-            pltpu.VMEM((4, STRIP, QUARTER), bf),
-            pltpu.VMEM((2,) + strip, bf),
+            pltpu.VMEM((4, 2, STRIP, QUARTER), bf),
             pltpu.VMEM((2, 16) + strip, bf),
             pltpu.VMEM((2, 4) + strip, bf),
             pltpu.VMEM((2, 2, STRIP, HALF), bf),
@@ -584,14 +637,15 @@
             pltpu.VMEM((2, 3) + strip, bf),
             pltpu.VMEM((2,) + strip, bf),
             pltpu.VMEM(strip, bf),
-            pltpu.VMEM((2,) + strip, bf),
-            pltpu.VMEM((4,) + strip, bf),
+            pltpu.VMEM((4, 2, STRIP, QUARTER), bf),
+            pltpu.VMEM((STRIP, QUARTER), bf),
+            pltpu.VMEM((2, STRIP, QUARTER), bf),
             pltpu.VMEM((4, 2, 2, 16, LANES), f32),
             pltpu.VMEM((4, 2, 2, 16, LANES), f32),
             pltpu.VMEM((2, 2, 16, LANES), f32),
             pltpu.VMEM((2, 16, LANES), f32),
             pltpu.VMEM((2, HALF, QUARTER), bf),
-            pltpu.VMEM((2, HALF, QUARTER), bf),
+            pltpu.VMEM((2, NZ, 2, STRIP, QUARTER), bf),
             pltpu.VMEM((2, 2, HALF // 2, WIDTH), bf),
             pltpu.VMEM((4, 4 * STRIP, QUARTER), bf),
             pltpu.VMEM((WIDTH, LANES), f32),
@@ -604,7 +658,8 @@
             pltpu.VMEM((2, LANES, HALF), bf),
             pltpu.SemaphoreType.DMA((N_SEM,)),
             pltpu.SemaphoreType.DMA((N_SEM,)),
-            pltpu.SemaphoreType.DMA((11,)),
+            pltpu.SemaphoreType.DMA((15,)),
+            pltpu.SemaphoreType.DMA((4,)),
             pltpu.SemaphoreType.DMA((16,)),
         ],
         compiler_params=pltpu.CompilerParams(

time: 110 us -> 105 us (0.955)
  Pallas kernels: 107 us -> 103 us
    pallas_call x1, Pallas kernels: 107 us -> 103 us  [local(): pl.pallas_call(kernel, out_shape=jax.ShapeDtypeStruct((WIDTH, WIDTH), bf)...]
where the time goes in v2:
time: 105 us
  Pallas kernels  103 us (98%)
  local copies, waits for them, and re-layouts  2.19 us (2%)
    pallas_call x1, Pallas kernels, local(): pl.pallas_call(kernel, out_shape=jax.ShapeDtypeStruct((WIDTH, WIDTH), bf)...  103 us
    unnamed x1, local copies, waits for them, and re-layouts  2.19 us

profile of v2, /device:TPU:3, one launch (start us, length us, event | category | flops | bytes accessed | tf_op | source)
XLA Modules:
  0.0 105.0 jit_solution(8796615013084970325)
XLA Ops:
  0.0 102.8 %shard_map.73 = bf16[1536,1536]{1,0:T(8,128)(2,1)S(1)} custom-call(s32[2]{0:T(128)} %owner_hbm.1, s32[2,4]{1,0:T(2,128)} %assign_hbm.1, bf16[48,1536]{1,0:T(8,128)(2,1)} %bitcast.11, bf16[2,48,1536]{2,1,0:T(8,128)(2,1)} %bitcast.10, bf16[2,16,48,1536]{3,2,1,0:T(8,128)(2,1)} %bitcast.9, bf16[2,16,1536]{2,1,0:T(8,128)(2,1)} %bitcast.12, bf16[2,1536]{1,0:T(2,128)(2,1)} %bitcast.13), custom_call_target="tpu_custom_call" | custom-call | flops 905969664 | bytes 10000000 | tf_op jit(solution)/shard_map/pallas_call | solution.py:620
  102.8 2.2 %copy.9 = bf16[1,1536,1536]{2,1,0:T(8,128)(2,1)} copy(bf16[1,1536,1536]{2,1,0:T(8,128)(2,1)S(1)} %bitcast.8) | data formatting | bytes 9437184

commit v3 on v2

--- a/solution.py
+++ b/solution.py
@@ -31,7 +31,7 @@
 
 def kernel(
     owner_hbm, assign_hbm, g_hbm, a_hbm, q_hbm, lg_hbm, la_hbm, out_ref,
-    owner_ref, assign_ref, lgv, lav, g, av, qv, qsel, qr_low, qr_high, qs, qt, qx, qc, aq, ac, ax, vsel, vy, vx, vc, fg, fa, fq, p, lgc, sc, bp, bo, bi, bk, bc, bt,
+    owner_ref, assign_ref, lgv, lav, g, av, qv, qsel, qr_low, qr_high, qs, qt, qx_low, qx_high, qc, aq, ac, ax, vsel, vy, vx, vc, fg, fa, fq, p, lgc, sc, bp, bo, bi, bk, bc, bt,
     ssem, rsem, lsem, a_recv, b_recv,
 ):
     member = lax.axis_index("grp")
@@ -168,19 +168,13 @@
             self.low(("dl", 1), down, x, z)
 
         def begin_high(self):
+            self.high(("xh", 0), across, x, z)
+            if self is gq:
+                self.paired = self.whole(x)
             self.high(("uh", 1), up, x, z)
             self.high(("dh", 1), down, x, z)
-            self.high(("xh", 0), across, x, z)
-            self.to_sibling(x, z)
-
-        def begin(self):
-            self.low(("x", 0), across, x, z)
-            self.high(("uh", 1), up, x, z)
-            self.high(("dh", 1), down, x, z)
-            self.low(("ul", 1), up, x, z)
-            self.low(("dl", 1), down, x, z)
-            self.high(("xh", 0), across, x, z)
-            self.paired = self.whole(x)
+            if self is not gq:
+                self.to_sibling(x, z)
 
         def whole(self, bx):
             m = number()
@@ -364,9 +358,11 @@
             qsel[layer, slot] = qv[layer, assign_ref[layer, slot]]
     y_up, y_down = (xh * 4 + (y + 1) % 4, dp), (xh * 4 + (y + 3) % 4, dp)
     far, above, below = (y + 2) % 4, (y + 1) % 4, (y + 3) % 4
-    m_q1, m_q2 = [number() for _ in range(2)], [number() for _ in range(2)]
+    m_q1, m_q2, m_q3 = ([number() for _ in range(2)] for _ in range(3))
     send(m_q1[0], qsel.at[:, far, :, :HALF], qr_low.at[:, 1], y_up)
     send(m_q1[1], qsel.at[:, far, :, HALF:], qr_high.at[:, 1], y_down)
+    send(m_q3[0], qsel.at[:, above, :, HALF:], qt.at[:, 1, :, HALF:], y_up)
+    send(m_q3[1], qsel.at[:, below, :, :HALF], qt.at[:, 2, :, :HALF], y_down)
     gg.begin()
 
     for layer in range(2):
@@ -380,14 +376,12 @@
 
     arrive(m_q1[0], qr_low.at[:, 1], y_down)
     for layer in range(2):
-        qs[0, layer, :, :HALF] = qr_low[layer, one_if(owners_y[layer] == below)]
-        qs[0, layer, :, HALF:] = qsel[layer, above, :, HALF:]
-    send(m_q2[0], qs.at[0], qt.at[:, 1], y_up)
+        qs[0, layer] = qr_low[layer, one_if(owners_y[layer] == below)]
+    send(m_q2[0], qs.at[0], qt.at[:, 1, :, :HALF], y_up)
     arrive(m_q1[1], qr_high.at[:, 1], y_up)
     for layer in range(2):
-        qs[1, layer, :, :HALF] = qsel[layer, below, :, :HALF]
-        qs[1, layer, :, HALF:] = qr_high[layer, one_if(owners_y[layer] == above)]
-    send(m_q2[1], qs.at[1], qt.at[:, 2], y_down)
+        qs[1, layer] = qr_high[layer, one_if(owners_y[layer] == above)]
+    send(m_q2[1], qs.at[1], qt.at[:, 2, :, HALF:], y_down)
 
     for k in range(1, 4):
         m_a = (y + k) % 4
@@ -444,10 +438,11 @@
 
     ring_a("u", 1, z)
     ring_a("d", 1, z)
-    gg.step(2)
-
-    arrive(m_q2[0], qt.at[:, 1], y_down)
-    arrive(m_q2[1], qt.at[:, 2], y_up)
+
+    arrive(m_q3[0], qt.at[:, 1, :, HALF:], y_down)
+    arrive(m_q3[1], qt.at[:, 2, :, :HALF], y_up)
+    arrive(m_q2[0], qt.at[:, 1, :, :HALF], y_down)
+    arrive(m_q2[1], qt.at[:, 2, :, HALF:], y_up)
     for k in range(1, 4):
         arrive(m_vy[k - 1], vy.at[(y + 4 - k) % 4], partner)
 
@@ -456,24 +451,28 @@
         by_below = (away >= 2) if column_half == 0 else (away == 3)
         return jnp.where(away == 0, 0, jnp.where(by_below, 1, 2))
 
-    m_qx, m_vx = number(), number()
+    m_qx, m_vx = [number() for _ in range(2)], number()
     for n in range(2):
         half = slice(n * HALF, (n + 1) * HALF)
-        qc[:, half] = qt[1 - xh, came(1 - xh, n), :, half]
-    send(m_qx, qc, qx.at[1], partner)
+        qc[n] = qt[1 - xh, came(1 - xh, n), :, half]
+        send(m_qx[n], qc.at[n], (qx_low, qx_high)[n].at[1], partner)
     vc[...] = vy[other_y, 1 - xh]
     send(m_vx, vc, vx.at[1], partner)
     for n in range(2):
         half = slice(n * HALF, (n + 1) * HALF)
-        qx[0, :, half] = qt[xh, came(xh, n), :, half]
+        (qx_low, qx_high)[n][0] = qt[xh, came(xh, n), :, half]
     vx[0] = vy[owner_y, xh]
+    gg.step(2)
 
     step_a(1)
     gg.step(3)
     step_a(2)
-    arrive(m_qx, qx.at[1], partner)
-    fq[c, x, strip_of(z), :] = qx[is_far]
-    gq.begin()
+    arrive(m_qx[0], qx_low.at[1], partner)
+    fq[c, x, strip_of(z), :HALF] = qx_low[is_far]
+    gq.begin_low()
+    arrive(m_qx[1], qx_high.at[1], partner)
+    fq[c, x, strip_of(z), HALF:] = qx_high[is_far]
+    gq.begin_high()
     step_a(3)
     gg.last()
     step_a(4)
@@ -633,10 +632,11 @@
             pltpu.VMEM((2, 4) + strip, bf),
             pltpu.VMEM((2, 2, STRIP, HALF), bf),
             pltpu.VMEM((2, 2, STRIP, HALF), bf),
-            pltpu.VMEM((2, 2) + strip, bf),
+            pltpu.VMEM((2, 2, STRIP, HALF), bf),
             pltpu.VMEM((2, 3) + strip, bf),
-            pltpu.VMEM((2,) + strip, bf),
-            pltpu.VMEM(strip, bf),
+            pltpu.VMEM((2, STRIP, HALF), bf),
+            pltpu.VMEM((2, STRIP, HALF), bf),
+            pltpu.VMEM((2, STRIP, HALF), bf),
             pltpu.VMEM((4, 2, STRIP, QUARTER), bf),
             pltpu.VMEM((STRIP, QUARTER), bf),
             pltpu.VMEM((2, STRIP, QUARTER), bf),

time: 105 us -> 103 us (0.981)
  Pallas kernels: 103 us -> 101 us
    pallas_call x1, Pallas kernels: 103 us -> 101 us  [local(): pl.pallas_call(kernel, out_shape=jax.ShapeDtypeStruct((WIDTH, WIDTH), bf)...]
where the time goes in v3:
time: 103 us
  Pallas kernels  101 us (98%)
  local copies, waits for them, and re-layouts  2.19 us (2%)
    pallas_call x1, Pallas kernels, local(): pl.pallas_call(kernel, out_shape=jax.ShapeDtypeStruct((WIDTH, WIDTH), bf)...  101 us
    unnamed x1, local copies, waits for them, and re-layouts  2.19 us

profile of v3, /device:TPU:3, one launch (start us, length us, event | category | flops | bytes accessed | tf_op | source)
XLA Modules:
  0.0 102.9 jit_solution(12641591130586456906)
XLA Ops:
  0.0 100.7 %shard_map.73 = bf16[1536,1536]{1,0:T(8,128)(2,1)S(1)} custom-call(s32[2]{0:T(128)} %owner_hbm.1, s32[2,4]{1,0:T(2,128)} %assign_hbm.1, bf16[48,1536]{1,0:T(8,128)(2,1)} %bitcast.11, bf16[2,48,1536]{2,1,0:T(8,128)(2,1)} %bitcast.10, bf16[2,16,48,1536]{3,2,1,0:T(8,128)(2,1)} %bitcast.9, bf16[2,16,1536]{2,1,0:T(8,128)(2,1)} %bitcast.12, bf16[2,1536]{1,0:T(2,128)(2,1)} %bitcast.13), custom_call_target="tpu_custom_call" | custom-call | flops 905969664 | bytes 10000000 | tf_op jit(solution)/shard_map/pallas_call | solution.py:619
  100.7 2.2 %copy.9 = bf16[1,1536,1536]{2,1,0:T(8,128)(2,1)} copy(bf16[1,1536,1536]{2,1,0:T(8,128)(2,1)S(1)} %bitcast.8) | data formatting | bytes 9437184

commit v4 on v3

--- a/solution.py
+++ b/solution.py
@@ -18,7 +18,7 @@
 HALF = WIDTH // 2
 QUARTER = WIDTH // 4
 TILE = 256
-N_SEM = 256
+N_SEM = 320
 
 
 def works(x, z):
@@ -436,8 +436,39 @@
         if s < 3:
             ring_a("d", s + 1, hi)
 
+    def blocks_a(s):
+        lo, hi = (z + NZ - s) % NZ, (z + s) % NZ
+        return (lo,) if s in (0, 4) else (lo, hi)
+
+    m_y = {}
+
+    def move_y(name, s, n, target, ref):
+        m_y[name, s, n] = number()
+        send(m_y[name, s, n], ref, ref, target)
+
+    def cross_y(s):
+        for n, bz in enumerate(blocks_a(s)):
+            ref = fa.at[y // 2, bz, y % 2]
+            move_y("u", s, n, y_up, ref)
+            move_y("d", s, n, y_down, ref)
+
+    def relay_y(s):
+        for n, bz in enumerate(blocks_a(s)):
+            from_below, from_above = fa.at[below // 2, bz, below % 2], fa.at[above // 2, bz, above % 2]
+            arrive(m_y["u", s, n], from_below, sibling)
+            if n == 0:
+                move_y("f", s, n, y_up, from_below)
+            arrive(m_y["d", s, n], from_above, sibling)
+            if n == 1:
+                move_y("f", s, n, y_down, from_above)
+
+    def finish_y(s):
+        for n, bz in enumerate(blocks_a(s)):
+            arrive(m_y["f", s, n], fa.at[far // 2, bz, far % 2], sibling)
+
     ring_a("u", 1, z)
     ring_a("d", 1, z)
+    cross_y(0)
 
     arrive(m_q3[0], qt.at[:, 1, :, HALF:], y_down)
     arrive(m_q3[1], qt.at[:, 2, :, :HALF], y_up)
@@ -465,8 +496,12 @@
     gg.step(2)
 
     step_a(1)
+    cross_y(1)
     gg.step(3)
+    relay_y(0)
     step_a(2)
+    cross_y(2)
+    relay_y(1)
     arrive(m_qx[0], qx_low.at[1], partner)
     fq[c, x, strip_of(z), :HALF] = qx_low[is_far]
     gq.begin_low()
@@ -474,25 +509,14 @@
     fq[c, x, strip_of(z), HALF:] = qx_high[is_far]
     gq.begin_high()
     step_a(3)
+    cross_y(3)
+    gq.swap()
+    step_a(4)
+    cross_y(4)
+    relay_y(2)
+    gq.from_x()
     gg.last()
-    step_a(4)
-    m_y1, m_y2 = [number() for _ in range(2)], [number() for _ in range(2)]
-    plane = fa.at[y // 2, :, y % 2]
-    send(m_y1[0], plane, plane, y_up)
-    send(m_y1[1], plane, plane, y_down)
-    gq.swap()
-    arrive(m_vx, vx.at[1], partner)
-    for n in range(WIDTH // LANES):
-        lg_row = vx[is_far, 0, n:n + 1, :]
-        lgc[n * LANES:(n + 1) * LANES, :] = jnp.transpose(jnp.broadcast_to(lg_row, (LANES, LANES)))
-    gq.from_x()
-    gq.step(1)
-    arrive(m_y1[0], fa.at[below // 2, :, below % 2], sibling)
-    lower = fa.at[below // 2, 0:4, below % 2]
-    send(m_y2[0], lower, lower, y_up)
-    arrive(m_y1[1], fa.at[above // 2, :, above % 2], sibling)
-    upper = fa.at[above // 2, 4:8, above % 2]
-    send(m_y2[1], upper, upper, y_down)
+    relay_y(3)
 
     arrive(*gq.paired, sibling)
     arrive(*gq.crossing, sibling)
@@ -507,11 +531,17 @@
     p_own, p_far = p.at[x * 2 + c], p.at[(1 - x) * 2 + c]
     send(m_p[0], p_own, p_own, across)
     send(m_p[1], p_own, p_own, sibling)
+    gq.step(1)
+    arrive(m_vx, vx.at[1], partner)
+    for n in range(WIDTH // LANES):
+        lg_row = vx[is_far, 0, n:n + 1, :]
+        lgc[n * LANES:(n + 1) * LANES, :] = jnp.transpose(jnp.broadcast_to(lg_row, (LANES, LANES)))
+    relay_y(4)
     arrive(m_p[0], p_far, across)
     send(m_p[2], p_far, p_far, sibling)
     gq.step(2)
-    arrive(m_y2[0], fa.at[far // 2, 0:4, far % 2], sibling)
-    arrive(m_y2[1], fa.at[far // 2, 4:8, far % 2], sibling)
+    for s in range(5):
+        finish_y(s)
 
     arrive(m_p[1], p.at[x * 2 + 1 - c], sibling)
     arrive(m_p[2], p.at[(1 - x) * 2 + 1 - c], sibling)

time: 103 us -> 101 us (0.981)
  Pallas kernels: 101 us -> 98.3 us
    pallas_call x1, Pallas kernels: 101 us -> 98.3 us  [local(): pl.pallas_call(kernel, out_shape=jax.ShapeDtypeStruct((WIDTH, WIDTH), bf)...]
where the time goes in v4:
time: 101 us
  Pallas kernels  98.3 us (97%)
  local copies, waits for them, and re-layouts  2.19 us (2%)
    pallas_call x1, Pallas kernels, local(): pl.pallas_call(kernel, out_shape=jax.ShapeDtypeStruct((WIDTH, WIDTH), bf)...  98.3 us
    unnamed x1, local copies, waits for them, and re-layouts  2.19 us

profile of v4, /device:TPU:3, one launch (start us, length us, event | category | flops | bytes accessed | tf_op | source)
XLA Modules:
  0.0 100.5 jit_solution(1163226504068193637)
XLA Ops:
  0.0 98.3 %shard_map.73 = bf16[1536,1536]{1,0:T(8,128)(2,1)S(1)} custom-call(s32[2]{0:T(128)} %owner_hbm.1, s32[2,4]{1,0:T(2,128)} %assign_hbm.1, bf16[48,1536]{1,0:T(8,128)(2,1)} %bitcast.11, bf16[2,48,1536]{2,1,0:T(8,128)(2,1)} %bitcast.10, bf16[2,16,48,1536]{3,2,1,0:T(8,128)(2,1)} %bitcast.9, bf16[2,16,1536]{2,1,0:T(8,128)(2,1)} %bitcast.12, bf16[2,1536]{1,0:T(2,128)(2,1)} %bitcast.13), custom_call_target="tpu_custom_call" | custom-call | flops 905969664 | bytes 10000000 | tf_op jit(solution)/shard_map/pallas_call | solution.py:649
  98.3 2.2 %copy.9 = bf16[1,1536,1536]{2,1,0:T(8,128)(2,1)} copy(bf16[1,1536,1536]{2,1,0:T(8,128)(2,1)S(1)} %bitcast.8) | data formatting | bytes 9437184

commit v5 on v4

--- a/solution.py
+++ b/solution.py
@@ -31,7 +31,7 @@
 
 def kernel(
     owner_hbm, assign_hbm, g_hbm, a_hbm, q_hbm, lg_hbm, la_hbm, out_ref,
-    owner_ref, assign_ref, lgv, lav, g, av, qv, qsel, qr_low, qr_high, qs, qt, qx_low, qx_high, qc, aq, ac, ax, vsel, vy, vx, vc, fg, fa, fq, p, lgc, sc, bp, bo, bi, bk, bc, bt,
+    owner_ref, assign_ref, lgv, lav, g, av, qv, qsel, qr_low, qr_high, qs, qt, qx_low, qx_high, qc, aq, ac, ax, vsel, vsb, vy, vx, vc, vf, fg, fa, fq, p, lgc, sc, bp, bo, bi, bk, bc, bt,
     ssem, rsem, lsem, a_recv, b_recv,
 ):
     member = lax.axis_index("grp")
@@ -72,14 +72,11 @@
     across = dev(xh, y, 1 - x, z, c)
     up = dev(xh, y, x, (z + 1) % NZ, c)
     down = dev(xh, y, x, (z + NZ - 1) % NZ, c)
-    across_other = dev(xh, y, 1 - x, z, 1 - c)
-    up_other = dev(xh, y, x, (z + 1) % NZ, 1 - c)
-    down_other = dev(xh, y, x, (z + NZ - 1) % NZ, 1 - c)
     partner = dev(1 - xh, y, x, z, c)
 
     barrier = pltpu.get_barrier_semaphore()
 
-    near = [up, down, up_other, down_other, partner]
+    near = [up, down, partner]
     near += [
         dev(xh, (y + k // 4) % 4, (x + k // 2) % 2, z, (c + k) % 2) for k in range(1, 16)
     ]
@@ -125,9 +122,9 @@
             pl.when(when)(landed.wait_recv)
 
     class Gather:
-        def __init__(self, ref, full, half=None, exists=None):
-            self.ref, self.full, self.cut, self.mid = ref, full, full // 2, full // 4
-            self.half = half or (lambda bx, bz, bc, to: ref(bx, bz, bc, 0, full))
+        def __init__(self, ref, full, exists=None, alone=False):
+            self.ref, self.full, self.cut, self.mid = ref, full, full // 2, 2 * LANES if alone else full // 4
+            self.alone = alone
             self.exists = exists or (lambda bx, bz: None)
             self.sib_waits = []
             self.m = {}
@@ -138,10 +135,12 @@
             return self.m[name]
 
         def to_sibling(self, bx, bz):
+            if self.alone:
+                return
             m = number()
-            ref = self.half(bx, bz, c, 1 - c)
+            ref = self.ref(bx, bz, c, 0, self.full)
             send(m, ref, ref, sibling, self.exists(bx, bz))
-            self.sib_waits.append((m, self.half(bx, bz, 1 - c, c), self.exists(bx, bz)))
+            self.sib_waits.append((m, self.ref(bx, bz, 1 - c, 0, self.full), self.exists(bx, bz)))
 
         def move(self, name, target, bx, bz, first, last):
             ref = self.ref(bx, bz, c, first, last)
@@ -169,18 +168,9 @@
 
         def begin_high(self):
             self.high(("xh", 0), across, x, z)
-            if self is gq:
-                self.paired = self.whole(x)
             self.high(("uh", 1), up, x, z)
             self.high(("dh", 1), down, x, z)
-            if self is not gq:
-                self.to_sibling(x, z)
-
-        def whole(self, bx):
-            m = number()
-            ref = self.ref(bx, z, c, 0, self.full)
-            send(m, ref, ref, sibling)
-            return m, self.ref(bx, z, 1 - c, 0, self.full)
+            self.to_sibling(x, z)
 
         def swap(self):
             self.wait_low(("x", 0), 1 - x, z)
@@ -189,10 +179,7 @@
 
         def from_x(self):
             self.wait_high(("xh", 0), 1 - x, z)
-            if self is gq:
-                self.crossing = self.whole(1 - x)
-            else:
-                self.to_sibling(1 - x, z)
+            self.to_sibling(1 - x, z)
 
         def step(self, s):
             lo, hi = (z + NZ - s) % NZ, (z + s) % NZ
@@ -213,16 +200,14 @@
                 self.low(("uq", s + 1), up, 1 - x, lo)
             else:
                 self.move(("uq", 4), up, 1 - x, lo, 0, self.mid)
-                self.move(("uc", 4), up_other, 1 - x, lo, 0, self.mid)
             self.wait_low(("dq", s), 1 - x, hi)
             if s < 3:
                 self.low(("dq", s + 1), down, 1 - x, hi)
             else:
                 self.move(("dq", 4), down, 1 - x, hi, self.mid, self.cut)
-                self.move(("dc", 4), down_other, 1 - x, hi, self.mid, self.cut)
             self.to_sibling(x, lo)
             self.to_sibling(x, hi)
-            if s == 2 and self is not gq:
+            if s == 2 and not self.alone:
                 self.from_x()
             if s > 1:
                 self.crossed(s - 1)
@@ -238,21 +223,17 @@
             far = (z + 4) % NZ
             self.wait_high(("uh", 4), x, far)
             self.high(("xu", 4), across, x, far)
-            self.high(("xc", 4), across_other, x, far)
             self.wait_low(("dl", 4), x, far)
             self.to_sibling(x, far)
             self.crossed(3)
             self.wait(("uq", 4), 1 - x, far, 0, self.mid)
             self.wait(("dq", 4), 1 - x, far, self.mid, self.cut)
             self.wait_high(("xu", 4), 1 - x, far)
+            self.to_sibling(1 - x, far)
 
         def end(self):
-            far = (z + 4) % NZ
             for m, ref, when in self.sib_waits:
                 arrive(m, ref, sibling, when)
-            self.wait(("uc", 4), 1 - x, far, 0, self.mid, 1 - c)
-            self.wait(("dc", 4), 1 - x, far, self.mid, self.cut, 1 - c)
-            self.wait(("xc", 4), 1 - x, far, self.cut, self.full, 1 - c)
 
     def strip_at(bz, bc):
         return pl.ds(pl.multiple_of((bz * 2 + bc) * STRIP, PIECE), STRIP)
@@ -262,9 +243,6 @@
 
     def at_z(bz):
         return pl.ds(pl.multiple_of(bz * 2 * STRIP, PIECE), 2 * STRIP)
-
-    def half_of(core):
-        return pl.ds(pl.multiple_of(core * HALF, LANES), HALF)
 
     class Ring:
         def __init__(self, f):
@@ -310,16 +288,15 @@
             self.wait("d", 4, 1, far)
 
     def by_strips(bx, bz, bc, first, last):
-        return fq.at[bc, bx, strip_of(bz), first:last]
+        cols = pl.ds(pl.multiple_of(bc * HALF + first, LANES), last - first)
+        return fq.at[:, bx, strip_of(bz), cols]
 
     def by_columns(bx, bz, bc, first, last):
         cols = pl.ds(pl.multiple_of(rank(bx, bz) * LANES, LANES), LANES)
         return out_ref.at[pl.ds(pl.multiple_of(bc * HALF + first, PIECE), last - first), cols]
 
     gg = Ring(fg)
-    gq = Gather(
-        by_strips, WIDTH, half=lambda bx, bz, bc, to: fq.at[bc, bx, strip_of(bz), half_of(to)]
-    )
+    gq = Gather(by_strips, HALF, alone=True)
     go = Gather(by_columns, HALF, exists=lambda bx, bz: works(bx, bz))
 
     own = pl.ds(pl.multiple_of(dp * STRIP, PIECE), STRIP)
@@ -413,10 +390,11 @@
                 cols = slice(n * LANES, (n + 1) * LANES)
                 vsel[slot, layer, 0, n:n + 1] = lg[:, cols]
                 vsel[slot, layer, 1, n:n + 1] = la_all[:, cols]
-    vy[y] = vsel[y]
+    vsb[...] = vsel[...].astype(jnp.bfloat16)
+    vy[y] = vsb[y]
     for k in range(1, 4):
         to = (y + k) % 4
-        send(m_vy[k - 1], vsel.at[to], vy.at[y], (xh * 4 + to, dp))
+        send(m_vy[k - 1], vsb.at[to], vy.at[y], (xh * 4 + to, dp))
     gg.step(1)
     arrive(m_ax, ax.at[1], partner)
     fa[y // 2, z, y % 2] = ax[is_far]
@@ -502,11 +480,16 @@
     step_a(2)
     cross_y(2)
     relay_y(1)
-    arrive(m_qx[0], qx_low.at[1], partner)
-    fq[c, x, strip_of(z), :HALF] = qx_low[is_far]
+    m_s = [number() for _ in range(3)]
+    for n, strip_half in enumerate((qx_low, qx_high)):
+        arrive(m_qx[n], strip_half.at[1], partner)
+        cols = slice(n * HALF, (n + 1) * HALF)
+        fq[c, x, strip_of(z), cols] = strip_half[is_far]
+        part = fq.at[c, x, strip_of(z), cols]
+        send(m_s[n], part, part, sibling)
+    for n in range(2):
+        arrive(m_s[n], fq.at[1 - c, x, strip_of(z), n * HALF:(n + 1) * HALF], sibling)
     gq.begin_low()
-    arrive(m_qx[1], qx_high.at[1], partner)
-    fq[c, x, strip_of(z), HALF:] = qx_high[is_far]
     gq.begin_high()
     step_a(3)
     cross_y(3)
@@ -515,11 +498,12 @@
     cross_y(4)
     relay_y(2)
     gq.from_x()
+    came_over = by_strips(1 - x, z, c, 0, HALF)
+    send(m_s[2], came_over, came_over, sibling)
     gg.last()
     relay_y(3)
 
-    arrive(*gq.paired, sibling)
-    arrive(*gq.crossing, sibling)
+    arrive(m_s[2], by_strips(1 - x, z, 1 - c, 0, HALF), sibling)
 
     def flat(value):
         return value.reshape((-1, value.shape[-1]))
@@ -533,8 +517,9 @@
     send(m_p[1], p_own, p_own, sibling)
     gq.step(1)
     arrive(m_vx, vx.at[1], partner)
+    vf[...] = vx[is_far].astype(jnp.float32)
     for n in range(WIDTH // LANES):
-        lg_row = vx[is_far, 0, n:n + 1, :]
+        lg_row = vf[0, n:n + 1, :]
         lgc[n * LANES:(n + 1) * LANES, :] = jnp.transpose(jnp.broadcast_to(lg_row, (LANES, LANES)))
     relay_y(4)
     arrive(m_p[0], p_far, across)
@@ -552,7 +537,7 @@
     lg_col = jnp.concatenate([lgc[pl.ds(pl.multiple_of(bx * HALF + (z * 2 + bc) * STRIP, PIECE), STRIP), :]
                               for bc in range(2) for bx in range(2)])
     for n in range(QUARTER // LANES):
-        la_row = vx[is_far, 1, pl.ds((x * 2 + c) * (QUARTER // LANES) + n, 1), :]
+        la_row = vf[1, pl.ds((x * 2 + c) * (QUARTER // LANES) + n, 1), :]
         cols = slice(n * LANES, (n + 1) * LANES)
         sc[:, cols] = (eigen[:, cols] / (lg_col * la_row + DAMPING)).astype(jnp.bfloat16)
 
@@ -612,7 +597,6 @@
             bt[c, :, cols] = jnp.transpose(total[cols, :]).astype(jnp.bfloat16)
 
     send(m_bt, bt.at[c], bt.at[c], sibling, is_worker)
-    gq.end()
     arrive(m_bt, bt.at[1 - c], sibling, is_worker)
 
     mine = pl.ds(pl.multiple_of(rank(x, z) * LANES, LANES), LANES)
@@ -671,8 +655,10 @@
             pltpu.VMEM((STRIP, QUARTER), bf),
             pltpu.VMEM((2, STRIP, QUARTER), bf),
             pltpu.VMEM((4, 2, 2, 16, LANES), f32),
-            pltpu.VMEM((4, 2, 2, 16, LANES), f32),
-            pltpu.VMEM((2, 2, 16, LANES), f32),
+            pltpu.VMEM((4, 2, 2, 16, LANES), bf),
+            pltpu.VMEM((4, 2, 2, 16, LANES), bf),
+            pltpu.VMEM((2, 2, 16, LANES), bf),
+            pltpu.VMEM((2, 16, LANES), bf),
             pltpu.VMEM((2, 16, LANES), f32),
             pltpu.VMEM((2, HALF, QUARTER), bf),
             pltpu.VMEM((2, NZ, 2, STRIP, QUARTER), bf),

time: 101 us -> 99.5 us (0.985)
  Pallas kernels: 98.3 us -> 96.8 us
    pallas_call x1, Pallas kernels: 98.3 us -> 96.8 us  [local(): pl.pallas_call(kernel, out_shape=jax.ShapeDtypeStruct((WIDTH, WIDTH), bf)...]
where the time goes in v5:
time: 99.5 us; the launch traced here: 98.9 us
  Pallas kernels  96.8 us (97%)
  local copies, waits for them, and re-layouts  2.19 us (2%)
    pallas_call x1, Pallas kernels, local(): pl.pallas_call(kernel, out_shape=jax.ShapeDtypeStruct((WIDTH, WIDTH), bf)...  96.8 us
    unnamed x1, local copies, waits for them, and re-layouts  2.19 us

profile of v5, /device:TPU:3, one launch (start us, length us, event | category | flops | bytes accessed | tf_op | source)
XLA Modules:
  0.0 98.9 jit_solution(14402763965746586842)
XLA Ops:
  0.0 96.8 %shard_map.73 = bf16[1536,1536]{1,0:T(8,128)(2,1)S(1)} custom-call(s32[2]{0:T(128)} %owner_hbm.1, s32[2,4]{1,0:T(2,128)} %assign_hbm.1, bf16[48,1536]{1,0:T(8,128)(2,1)} %bitcast.11, bf16[2,48,1536]{2,1,0:T(8,128)(2,1)} %bitcast.10, bf16[2,16,48,1536]{3,2,1,0:T(8,128)(2,1)} %bitcast.9, bf16[2,16,1536]{2,1,0:T(8,128)(2,1)} %bitcast.12, bf16[2,1536]{1,0:T(2,128)(2,1)} %bitcast.13), custom_call_target="tpu_custom_call" | custom-call | flops 905969664 | bytes 10000000 | tf_op jit(solution)/shard_map/pallas_call | solution.py:633
  96.8 2.2 %copy.9 = bf16[1,1536,1536]{2,1,0:T(8,128)(2,1)} copy(bf16[1,1536,1536]{2,1,0:T(8,128)(2,1)S(1)} %bitcast.8) | data formatting | bytes 9437184

commit v6 on v5

--- a/solution.py
+++ b/solution.py
@@ -301,6 +301,10 @@
 
     own = pl.ds(pl.multiple_of(dp * STRIP, PIECE), STRIP)
 
+    for load in load_g:
+        load.wait()
+    gg.share(g)
+
     for load in load_a:
         load.wait()
     mine_a = x * 2 + c
@@ -317,10 +321,6 @@
     @pl.when(in_place)
     def _():
         aq[y] = av[y]
-
-    for load in load_g:
-        load.wait()
-    gg.share(g)
 
     for load in loads:
         load.wait()
@@ -379,6 +379,7 @@
     send(m_ax, ac, ax.at[1], partner)
     ax[0] = aq[owner_y, xh]
 
+    gg.step(1)
     m_vy = [number() for _ in range(3)]
     for layer in range(2):
         la_all = lav[...].astype(jnp.float32)[layer:layer + 1]
@@ -395,7 +396,6 @@
     for k in range(1, 4):
         to = (y + k) % 4
         send(m_vy[k - 1], vsb.at[to], vy.at[y], (xh * 4 + to, dp))
-    gg.step(1)
     arrive(m_ax, ax.at[1], partner)
     fa[y // 2, z, y % 2] = ax[is_far]
     m_a = {}
@@ -447,6 +447,8 @@
     ring_a("u", 1, z)
     ring_a("d", 1, z)
     cross_y(0)
+    gg.step(2)
+
 
     arrive(m_q3[0], qt.at[:, 1, :, HALF:], y_down)
     arrive(m_q3[1], qt.at[:, 2, :, :HALF], y_up)
@@ -471,8 +473,6 @@
         half = slice(n * HALF, (n + 1) * HALF)
         (qx_low, qx_high)[n][0] = qt[xh, came(xh, n), :, half]
     vx[0] = vy[owner_y, xh]
-    gg.step(2)
-
     step_a(1)
     cross_y(1)
     gg.step(3)
@@ -480,6 +480,7 @@
     step_a(2)
     cross_y(2)
     relay_y(1)
+    gg.last()
     m_s = [number() for _ in range(3)]
     for n, strip_half in enumerate((qx_low, qx_high)):
         arrive(m_qx[n], strip_half.at[1], partner)
@@ -500,7 +501,6 @@
     gq.from_x()
     came_over = by_strips(1 - x, z, c, 0, HALF)
     send(m_s[2], came_over, came_over, sibling)
-    gg.last()
     relay_y(3)
 
     arrive(m_s[2], by_strips(1 - x, z, 1 - c, 0, HALF), sibling)

time: 99.5 us -> 101 us (1.015)
  Pallas kernels: 96.8 us -> 98.5 us
    pallas_call x1, Pallas kernels: 96.8 us -> 98.5 us  [local(): pl.pallas_call(kernel, out_shape=jax.ShapeDtypeStruct((WIDTH, WIDTH), bf)...]
where the time goes in v6:
time: 101 us
  Pallas kernels  98.5 us (98%)
  local copies, waits for them, and re-layouts  2.19 us (2%)
    pallas_call x1, Pallas kernels, local(): pl.pallas_call(kernel, out_shape=jax.ShapeDtypeStruct((WIDTH, WIDTH), bf)...  98.5 us
    unnamed x1, local copies, waits for them, and re-layouts  2.19 us

profile of v6, /device:TPU:3, one launch (start us, length us, event | category | flops | bytes accessed | tf_op | source)
XLA Modules:
  0.0 100.7 jit_solution(8599263184154216960)
XLA Ops:
  0.0 98.5 %shard_map.73 = bf16[1536,1536]{1,0:T(8,128)(2,1)S(1)} custom-call(s32[2]{0:T(128)} %owner_hbm.1, s32[2,4]{1,0:T(2,128)} %assign_hbm.1, bf16[48,1536]{1,0:T(8,128)(2,1)} %bitcast.11, bf16[2,48,1536]{2,1,0:T(8,128)(2,1)} %bitcast.10, bf16[2,16,48,1536]{3,2,1,0:T(8,128)(2,1)} %bitcast.9, bf16[2,16,1536]{2,1,0:T(8,128)(2,1)} %bitcast.12, bf16[2,1536]{1,0:T(2,128)(2,1)} %bitcast.13), custom_call_target="tpu_custom_call" | custom-call | flops 905969664 | bytes 10000000 | tf_op jit(solution)/shard_map/pallas_call | solution.py:633
  98.5 2.2 %copy.9 = bf16[1,1536,1536]{2,1,0:T(8,128)(2,1)} copy(bf16[1,1536,1536]{2,1,0:T(8,128)(2,1)S(1)} %bitcast.8) | data formatting | bytes 9437184

commit v7 on v5

--- a/solution.py
+++ b/solution.py
@@ -82,6 +82,41 @@
     ]
     for target in near:
         pl.semaphore_signal(barrier, inc=1, device_id=target, device_id_type=MESH)
+
+    y_up, y_down = (xh * 4 + (y + 1) % 4, dp), (xh * 4 + (y + 3) % 4, dp)
+    far, above, below = (y + 2) % 4, (y + 1) % 4, (y + 3) % 4
+    for load in load_a:
+        load.wait()
+    for load in load_g:
+        load.wait()
+    for load in loads:
+        load.wait()
+    owner = owner_ref[xh]
+    other = owner_ref[1 - xh]
+    is_far = lax.bitwise_xor(lax.shift_right_logical(owner, 2), xh)
+    owner_y = lax.bitwise_and(owner, 3)
+    other_y = lax.bitwise_and(other, 3)
+    load_q.wait()
+    for layer in range(2):
+        for slot in range(4):
+            qsel[layer, slot] = qv[layer, assign_ref[layer, slot]]
+    for layer in range(2):
+        qr_low[layer, 0] = qsel[layer, above, :, :HALF]
+        qr_high[layer, 0] = qsel[layer, below, :, HALF:]
+        qt[layer, 0] = qsel[layer, y]
+    for layer in range(2):
+        la_all = lav[...].astype(jnp.float32)[layer:layer + 1]
+        lg_all = lgv[layer].astype(jnp.float32)
+        at_row = lax.broadcasted_iota(jnp.int32, lg_all.shape, 0)
+        for slot in range(4):
+            lg = jnp.sum(jnp.where(at_row == assign_ref[layer, slot], lg_all, 0.0), axis=0, keepdims=True)
+            for n in range(WIDTH // LANES):
+                cols = slice(n * LANES, (n + 1) * LANES)
+                vsel[slot, layer, 0, n:n + 1] = lg[:, cols]
+                vsel[slot, layer, 1, n:n + 1] = la_all[:, cols]
+    vsb[...] = vsel[...].astype(jnp.bfloat16)
+    vy[y] = vsb[y]
+
     pl.semaphore_wait(barrier, len(near))
 
     count = [0]
@@ -301,8 +336,6 @@
 
     own = pl.ds(pl.multiple_of(dp * STRIP, PIECE), STRIP)
 
-    for load in load_a:
-        load.wait()
     mine_a = x * 2 + c
     in_place = mine_a == y
     for n in range(4):
@@ -318,23 +351,8 @@
     def _():
         aq[y] = av[y]
 
-    for load in load_g:
-        load.wait()
     gg.share(g)
 
-    for load in loads:
-        load.wait()
-    owner = owner_ref[xh]
-    other = owner_ref[1 - xh]
-    is_far = lax.bitwise_xor(lax.shift_right_logical(owner, 2), xh)
-    owner_y = lax.bitwise_and(owner, 3)
-    other_y = lax.bitwise_and(other, 3)
-    load_q.wait()
-    for layer in range(2):
-        for slot in range(4):
-            qsel[layer, slot] = qv[layer, assign_ref[layer, slot]]
-    y_up, y_down = (xh * 4 + (y + 1) % 4, dp), (xh * 4 + (y + 3) % 4, dp)
-    far, above, below = (y + 2) % 4, (y + 1) % 4, (y + 3) % 4
     m_q1, m_q2, m_q3 = ([number() for _ in range(2)] for _ in range(3))
     send(m_q1[0], qsel.at[:, far, :, :HALF], qr_low.at[:, 1], y_up)
     send(m_q1[1], qsel.at[:, far, :, HALF:], qr_high.at[:, 1], y_down)
@@ -342,10 +360,6 @@
     send(m_q3[1], qsel.at[:, below, :, :HALF], qt.at[:, 2, :, :HALF], y_down)
     gg.begin()
 
-    for layer in range(2):
-        qr_low[layer, 0] = qsel[layer, above, :, :HALF]
-        qr_high[layer, 0] = qsel[layer, below, :, HALF:]
-        qt[layer, 0] = qsel[layer, y]
     owners_y = [lax.bitwise_and(owner_ref[layer], 3) for layer in range(2)]
 
     def one_if(condition):
@@ -380,18 +394,6 @@
     ax[0] = aq[owner_y, xh]
 
     m_vy = [number() for _ in range(3)]
-    for layer in range(2):
-        la_all = lav[...].astype(jnp.float32)[layer:layer + 1]
-        lg_all = lgv[layer].astype(jnp.float32)
-        at_row = lax.broadcasted_iota(jnp.int32, lg_all.shape, 0)
-        for slot in range(4):
-            lg = jnp.sum(jnp.where(at_row == assign_ref[layer, slot], lg_all, 0.0), axis=0, keepdims=True)
-            for n in range(WIDTH // LANES):
-                cols = slice(n * LANES, (n + 1) * LANES)
-                vsel[slot, layer, 0, n:n + 1] = lg[:, cols]
-                vsel[slot, layer, 1, n:n + 1] = la_all[:, cols]
-    vsb[...] = vsel[...].astype(jnp.bfloat16)
-    vy[y] = vsb[y]
     for k in range(1, 4):
         to = (y + k) % 4
         send(m_vy[k - 1], vsb.at[to], vy.at[y], (xh * 4 + to, dp))

time: 99.5 us -> 98.7 us (level)
  no operation moved by 1% of the time
where the time goes in v7:
time: 98.7 us; the launch traced here: 98.5 us
  Pallas kernels  96.3 us (98%)
  local copies, waits for them, and re-layouts  2.19 us (2%)
    pallas_call x1, Pallas kernels, local(): pl.pallas_call(kernel, out_shape=jax.ShapeDtypeStruct((WIDTH, WIDTH), bf)...  96.3 us
    unnamed x1, local copies, waits for them, and re-layouts  2.19 us

profile of v7, /device:TPU:3, one launch (start us, length us, event | category | flops | bytes accessed | tf_op | source)
XLA Modules:
  0.0 98.5 jit_solution(10762873724546966440)
XLA Ops:
  0.0 96.3 %shard_map.73 = bf16[1536,1536]{1,0:T(8,128)(2,1)S(1)} custom-call(s32[2]{0:T(128)} %owner_hbm.1, s32[2,4]{1,0:T(2,128)} %assign_hbm.1, bf16[48,1536]{1,0:T(8,128)(2,1)} %bitcast.11, bf16[2,48,1536]{2,1,0:T(8,128)(2,1)} %bitcast.10, bf16[2,16,48,1536]{3,2,1,0:T(8,128)(2,1)} %bitcast.9, bf16[2,16,1536]{2,1,0:T(8,128)(2,1)} %bitcast.12, bf16[2,1536]{1,0:T(2,128)(2,1)} %bitcast.13), custom_call_target="tpu_custom_call" | custom-call | flops 905969664 | bytes 10000000 | tf_op jit(solution)/shard_map/pallas_call | solution.py:635
  96.3 2.2 %copy.9 = bf16[1,1536,1536]{2,1,0:T(8,128)(2,1)} copy(bf16[1,1536,1536]{2,1,0:T(8,128)(2,1)S(1)} %bitcast.8) | data formatting | bytes 9437184

commit v8 on v7

--- a/solution.py
+++ b/solution.py
@@ -31,7 +31,7 @@
 
 def kernel(
     owner_hbm, assign_hbm, g_hbm, a_hbm, q_hbm, lg_hbm, la_hbm, out_ref,
-    owner_ref, assign_ref, lgv, lav, g, av, qv, qsel, qr_low, qr_high, qs, qt, qx_low, qx_high, qc, aq, ac, ax, vsel, vsb, vy, vx, vc, vf, fg, fa, fq, p, lgc, sc, bp, bo, bi, bk, bc, bt,
+    owner_ref, assign_ref, lgv, lav, g, av, qv, qsel, qr_low, qr_high, qs, qt, qx_low, qx_high, qc, aq, ac, ax, vsel, vsb, vy, vx, vc, vf, fg, fa, fq, p, lgc, sc, bp, bo, bi, bk, bc, bt, acc,
     ssem, rsem, lsem, a_recv, b_recv,
 ):
     member = lax.axis_index("grp")
@@ -599,6 +599,15 @@
             bt[c, :, cols] = jnp.transpose(total[cols, :]).astype(jnp.bfloat16)
 
     send(m_bt, bt.at[c], bt.at[c], sibling, is_worker)
+
+    def rows_at(n):
+        return pl.ds(pl.multiple_of(c * HALF + n * QUARTER, LANES), QUARTER)
+
+    @pl.when(is_worker)
+    def _():
+        for n in range(2):
+            acc[n] = jnp.dot(bt[c], flat(fq[c, :, :, rows_at(n)]), preferred_element_type=jnp.float32)
+
     arrive(m_bt, bt.at[1 - c], sibling, is_worker)
 
     mine = pl.ds(pl.multiple_of(rank(x, z) * LANES, LANES), LANES)
@@ -606,17 +615,16 @@
     def finish(n):
         @pl.when(is_worker)
         def _():
-            rows = pl.ds(pl.multiple_of(c * HALF + n * QUARTER, LANES), QUARTER)
-            part = sum(
-                jnp.dot(bt[k], flat(fq[k, :, :, rows]), preferred_element_type=jnp.float32) for k in range(2)
-            )
+            rows = rows_at(n)
+            part = acc[n] + jnp.dot(bt[1 - c], flat(fq[1 - c, :, :, rows]), preferred_element_type=jnp.float32)
             out_ref[rows, mine] = jnp.transpose(part).astype(jnp.bfloat16)
 
+    older = len(pending)
     finish(0)
     go.begin_low()
     finish(1)
     go.begin_high()
-    drain()
+    drain(older)
     go.swap()
     go.step(1)
     early = len(pending)
@@ -674,6 +682,7 @@
             pltpu.VMEM((12, 2, STRIP, LANES), bf),
             pltpu.VMEM((2, 2, HALF // 2, LANES), bf),
             pltpu.VMEM((2, LANES, HALF), bf),
+            pltpu.VMEM((2, LANES, QUARTER), f32),
             pltpu.SemaphoreType.DMA((N_SEM,)),
             pltpu.SemaphoreType.DMA((N_SEM,)),
             pltpu.SemaphoreType.DMA((15,)),

time: 98.7 us -> 100 us (1.013)
  Pallas kernels: 96.3 us -> 97.8 us
    pallas_call x1, Pallas kernels: 96.3 us -> 97.8 us  [local(): pl.pallas_call(kernel, out_shape=jax.ShapeDtypeStruct((WIDTH, WIDTH), bf)...]
where the time goes in v8:
time: 100 us
  Pallas kernels  97.8 us (98%)
  local copies, waits for them, and re-layouts  2.19 us (2%)
    pallas_call x1, Pallas kernels, local(): pl.pallas_call(kernel, out_shape=jax.ShapeDtypeStruct((WIDTH, WIDTH), bf)...  97.8 us
    unnamed x1, local copies, waits for them, and re-layouts  2.19 us

profile of v8, /device:TPU:3, one launch (start us, length us, event | category | flops | bytes accessed | tf_op | source)
XLA Modules:
  0.0 100.0 jit_solution(12871562341043134734)
XLA Ops:
  0.0 97.8 %shard_map.73 = bf16[1536,1536]{1,0:T(8,128)(2,1)S(1)} custom-call(s32[2]{0:T(128)} %owner_hbm.1, s32[2,4]{1,0:T(2,128)} %assign_hbm.1, bf16[48,1536]{1,0:T(8,128)(2,1)} %bitcast.11, bf16[2,48,1536]{2,1,0:T(8,128)(2,1)} %bitcast.10, bf16[2,16,48,1536]{3,2,1,0:T(8,128)(2,1)} %bitcast.9, bf16[2,16,1536]{2,1,0:T(8,128)(2,1)} %bitcast.12, bf16[2,1536]{1,0:T(2,128)(2,1)} %bitcast.13), custom_call_target="tpu_custom_call" | custom-call | flops 905969664 | bytes 10000000 | tf_op jit(solution)/shard_map/pallas_call | solution.py:643
  97.8 2.2 %copy.9 = bf16[1,1536,1536]{2,1,0:T(8,128)(2,1)} copy(bf16[1,1536,1536]{2,1,0:T(8,128)(2,1)S(1)} %bitcast.8) | data formatting | bytes 9437184

commit v9 on v7

--- a/solution.py
+++ b/solution.py
@@ -553,7 +553,6 @@
             bo[:, :, :, cols] = part.astype(jnp.bfloat16)
     m_b = number()
     send(m_b, bo.at[1 - c], bi, sibling)
-    gq.step(3)
     arrive(m_b, bi, sibling)
     done = (bp[c] + bi[...].astype(jnp.float32)).astype(jnp.bfloat16)
     for j in range(WIDTH // LANES):
@@ -577,6 +576,7 @@
             def _():
                 bc[x, :, strip_of(z), :] = part[...]
 
+    gq.step(3)
     gq.last()
     is_worker = works(x, z)
     m_bt = number()

time: 98.7 us -> 101 us (1.023)
  Pallas kernels: 96.3 us -> 98.3 us
    pallas_call x1, Pallas kernels: 96.3 us -> 98.3 us  [local(): pl.pallas_call(kernel, out_shape=jax.ShapeDtypeStruct((WIDTH, WIDTH), bf)...]
where the time goes in v9:
time: 101 us; the launch traced here: 100 us
  Pallas kernels  98.3 us (97%)
  local copies, waits for them, and re-layouts  2.19 us (2%)
    pallas_call x1, Pallas kernels, local(): pl.pallas_call(kernel, out_shape=jax.ShapeDtypeStruct((WIDTH, WIDTH), bf)...  98.3 us
    unnamed x1, local copies, waits for them, and re-layouts  2.19 us

profile of v9, /device:TPU:3, one launch (start us, length us, event | category | flops | bytes accessed | tf_op | source)
XLA Modules:
  0.0 100.5 jit_solution(8979598555107030439)
XLA Ops:
  0.0 98.3 %shard_map.73 = bf16[1536,1536]{1,0:T(8,128)(2,1)S(1)} custom-call(s32[2]{0:T(128)} %owner_hbm.1, s32[2,4]{1,0:T(2,128)} %assign_hbm.1, bf16[48,1536]{1,0:T(8,128)(2,1)} %bitcast.11, bf16[2,48,1536]{2,1,0:T(8,128)(2,1)} %bitcast.10, bf16[2,16,48,1536]{3,2,1,0:T(8,128)(2,1)} %bitcast.9, bf16[2,16,1536]{2,1,0:T(8,128)(2,1)} %bitcast.12, bf16[2,1536]{1,0:T(2,128)(2,1)} %bitcast.13), custom_call_target="tpu_custom_call" | custom-call | flops 905969664 | bytes 10000000 | tf_op jit(solution)/shard_map/pallas_call | solution.py:635
  98.3 2.2 %copy.9 = bf16[1,1536,1536]{2,1,0:T(8,128)(2,1)} copy(bf16[1,1536,1536]{2,1,0:T(8,128)(2,1)S(1)} %bitcast.8) | data formatting | bytes 9437184

commit v10 on v7

--- a/solution.py
+++ b/solution.py
@@ -504,6 +504,7 @@
     send(m_s[2], came_over, came_over, sibling)
     gg.last()
     relay_y(3)
+    gq.step(1)
 
     arrive(m_s[2], by_strips(1 - x, z, 1 - c, 0, HALF), sibling)
 
@@ -517,7 +518,6 @@
     p_own, p_far = p.at[x * 2 + c], p.at[(1 - x) * 2 + c]
     send(m_p[0], p_own, p_own, across)
     send(m_p[1], p_own, p_own, sibling)
-    gq.step(1)
     arrive(m_vx, vx.at[1], partner)
     vf[...] = vx[is_far].astype(jnp.float32)
     for n in range(WIDTH // LANES):

time: 98.7 us -> 101 us (1.023)
  Pallas kernels: 96.3 us -> 99 us
    pallas_call x1, Pallas kernels: 96.3 us -> 99 us  [local(): pl.pallas_call(kernel, out_shape=jax.ShapeDtypeStruct((WIDTH, WIDTH), bf)...]
where the time goes in v10:
time: 101 us
  Pallas kernels  99 us (98%)
  local copies, waits for them, and re-layouts  2.19 us (2%)
    pallas_call x1, Pallas kernels, local(): pl.pallas_call(kernel, out_shape=jax.ShapeDtypeStruct((WIDTH, WIDTH), bf)...  99 us
    unnamed x1, local copies, waits for them, and re-layouts  2.19 us

profile of v10, /device:TPU:3, one launch (start us, length us, event | category | flops | bytes accessed | tf_op | source)
XLA Modules:
  0.0 101.2 jit_solution(5931085235160687554)
XLA Ops:
  0.0 99.0 %shard_map.73 = bf16[1536,1536]{1,0:T(8,128)(2,1)S(1)} custom-call(s32[2]{0:T(128)} %owner_hbm.1, s32[2,4]{1,0:T(2,128)} %assign_hbm.1, bf16[48,1536]{1,0:T(8,128)(2,1)} %bitcast.11, bf16[2,48,1536]{2,1,0:T(8,128)(2,1)} %bitcast.10, bf16[2,16,48,1536]{3,2,1,0:T(8,128)(2,1)} %bitcast.9, bf16[2,16,1536]{2,1,0:T(8,128)(2,1)} %bitcast.12, bf16[2,1536]{1,0:T(2,128)(2,1)} %bitcast.13), custom_call_target="tpu_custom_call" | custom-call | flops 905969664 | bytes 10000000 | tf_op jit(solution)/shard_map/pallas_call | solution.py:635
  99.0 2.2 %copy.9 = bf16[1,1536,1536]{2,1,0:T(8,128)(2,1)} copy(bf16[1,1536,1536]{2,1,0:T(8,128)(2,1)S(1)} %bitcast.8) | data formatting | bytes 9437184
